TPU v7x, 128 devices: a whole 4x4x4 slice. The times are simulated.
128 devices in a mesh: gx: 32 (over x, z, core), gy: 4 (over y).
Axes of the slice: x: 4, y: 4, z: 4, core: 2. Of those that a mesh axis runs over, the one named last changes fastest.
Arguments:
- point_feats: bfloat16 [4096, 32, 128], P(('gx', 'gy')), may hold values from -6 to 6
- point_offsets: bfloat16 [4096, 3, 128], P(('gx', 'gy')), may hold values from 0 to 1
- base_cells: int32 [4096, 128], P(('gx', 'gy')), may hold values from 0 to 1784
- block_owners: int32 [4096, 1], P(('gx', 'gy')), may hold values from 0 to 31; in each aligned block of 32 rows (0 to 31, 32 to 63, ...) at most 2 rows name the same one
- point_counts: int32 [128], P(('gx', 'gy')), may hold values from 1 to 4096, 393216 in all
- lift_weight: bfloat16 [32, 32], replicated, may hold values from -1 to 1
- conv_weight: bfloat16 [27, 32, 32], replicated, may hold values from -0.21875 to 0.21875
- read_weight: bfloat16 [32], replicated, may hold values from -1 to 1
- cotangent: float32 [4096, 128], P(('gx', 'gy')), may hold values from -24 to 24
Outputs:
- prediction: float32 [4096, 128], P(('gx', 'gy'))
- grad_feats: bfloat16 [4096, 32, 128], P(('gx', 'gy'))
- grad_conv: float32 [27, 32, 32], replicated
Inputs may be any that keep to these rules, and one draw needn't show every extreme that they name: `block_owners`: among the blocks of one device, at most 2 name the same owner; some owner is named by exactly 2 of them. `point_counts`: the counts sum to 393216; one device is full.
All inputs are finite; a program needn't handle non-finite values.
Results may differ from a plain program's by a relative error of at most 0.015.
Values may be sent and summed in bfloat16 or wider, within the bound.
A program may use at most 64 MiB of HBM per device.

v0:
```python
import math

import jax
import jax.numpy as jnp
from jax import lax
from jax.sharding import PartitionSpec as P

CX = 2
CY = 8
NZ = 256


width_sq = 0.5


def padded_2(cells, sides, width):
    for axis, dim in sides:
        count = lax.axis_size(axis)
        ends = count - 1
        head = lax.slice_in_dim(cells, 0, width, axis=dim)
        tail = lax.slice_in_dim(cells, cells.shape[dim] - width, cells.shape[dim], axis=dim)
        cells = jnp.concatenate(
            [
                lax.ppermute(tail, axis, [(i, (i + 1) % count) for i in range(ends)]),
                cells,
                lax.ppermute(head, axis, [((i + 1) % count, i) for i in range(ends)]),
            ],
            axis=dim,
        )
    return cells


def point_factors(offsets, base, slab_x, slab_y, depth):
    spots = offsets.astype(jnp.float32)
    inner = (slab_y - 1) * (depth - 1)
    corner_a = base // inner
    corner_b = base // (depth - 1) % (slab_y - 1)
    corner_c = base % (depth - 1)
    near_x = jnp.exp(-spots[:, 0, :] ** 2 / width_sq)
    far_x = jnp.exp(-((spots[:, 0, :] - 1.0) ** 2) / width_sq)
    near_y = jnp.exp(-spots[:, 1, :] ** 2 / width_sq)
    far_y = jnp.exp(-((spots[:, 1, :] - 1.0) ** 2) / width_sq)
    near_z = jnp.exp(-spots[:, 2, :] ** 2 / width_sq)
    far_z = jnp.exp(-((spots[:, 2, :] - 1.0) ** 2) / width_sq)
    columns = jnp.arange(slab_x * slab_y, dtype=jnp.int32)[None, None, :]
    home = (corner_a * slab_y + corner_b)[:, :, None]
    plane = jnp.where(columns == home, (near_x * near_y)[:, :, None], 0.0)
    plane = plane + jnp.where(columns == home + 1, (near_x * far_y)[:, :, None], 0.0)
    plane = plane + jnp.where(columns == home + slab_y, (far_x * near_y)[:, :, None], 0.0)
    plane = plane + jnp.where(columns == home + slab_y + 1, (far_x * far_y)[:, :, None], 0.0)
    return (plane, near_z, far_z, corner_c)


def group_size(slots, block_len):
    return math.gcd(slots, max(1, 1024 // block_len))


def level_onehots(corner_c, depth):
    levels = jnp.arange(depth, dtype=jnp.int32)[None, None, :]
    lower = (levels == corner_c[:, :, None]).astype(jnp.bfloat16)
    upper = (levels == corner_c[:, :, None] + 1).astype(jnp.bfloat16)
    return (lower, upper)


def split_pair(values):
    high = values.astype(jnp.bfloat16)
    low = (values - high.astype(jnp.float32)).astype(jnp.bfloat16)
    return (high, low)


def spread_dense(values, factors, depth):
    plane, near_z, far_z, corner_c = factors
    slots, channels, block_len = values.shape
    columns = plane.shape[2]
    group = group_size(slots, block_len)
    turns = slots // group
    vals_g = values.reshape(turns, group, channels, block_len)
    plane_g = plane.reshape(turns, group, block_len, columns)
    near_g = near_z.reshape(turns, group, block_len)
    far_g = far_z.reshape(turns, group, block_len)
    level_g = corner_c.reshape(turns, group, block_len)

    def add_group(total, pieces):
        vals, flat_plane, near_f, far_f, level_c = pieces
        based = jnp.einsum("scb,sbk->cksb", vals, flat_plane, precision=lax.Precision.HIGHEST)
        lower, upper = level_onehots(level_c, depth)
        for factor, onehot in ((near_f, lower), (far_f, upper)):
            part = (based * factor[None, None]).reshape(channels * columns, group * block_len)
            high, low = split_pair(part)
            right = onehot.reshape(group * block_len, depth)
            total = total + jnp.dot(high, right, preferred_element_type=jnp.float32)
            total = total + jnp.dot(low, right, preferred_element_type=jnp.float32)
        return (total, None)

    start = jnp.zeros((channels * columns, depth), jnp.float32)
    total, unused = lax.scan(add_group, start, (vals_g, plane_g, near_g, far_g, level_g))
    return total.reshape(channels, columns * depth)


def sample_dense(field, factors, depth):
    plane, near_z, far_z, corner_c = factors
    channels = field.shape[0]
    slots, block_len, columns = plane.shape
    if field.dtype == jnp.bfloat16:
        parts = (field.reshape(channels, columns, depth),)
    else:
        parts = split_pair(field.reshape(channels, columns, depth))
    group = group_size(slots, block_len)
    turns = slots // group
    plane_g = plane.reshape(turns, group, block_len, columns)
    near_g = near_z.reshape(turns, group, block_len)
    far_g = far_z.reshape(turns, group, block_len)
    level_g = corner_c.reshape(turns, group, block_len)

    def read_group(carry, pieces):
        flat_plane, near_f, far_f, level_c = pieces
        lower, upper = level_onehots(level_c, depth)
        picked_low = sum(
            (
                jnp.einsum("ckd,sbd->cksb", part, lower, preferred_element_type=jnp.float32)
                for part in parts
            )
        )
        picked_up = sum(
            (
                jnp.einsum("ckd,sbd->cksb", part, upper, preferred_element_type=jnp.float32)
                for part in parts
            )
        )
        along = picked_low * near_f[None, None] + picked_up * far_f[None, None]
        return (
            carry,
            jnp.einsum("cksb,sbk->scb", along, flat_plane, precision=lax.Precision.HIGHEST),
        )

    unused, result = lax.scan(read_group, 0, (plane_g, near_g, far_g, level_g))
    return result.reshape(slots, channels, block_len)


def stack_taps(padded, step_x, size_x, size_y, size_z):
    return jnp.concatenate(
        [
            padded[:, step_x : step_x + size_x, step_y : step_y + size_y, step_z : step_z + size_z]
            for step_y in range(3)
            for step_z in range(3)
        ],
        axis=0,
    )


def convolve(padded, kernel, size_x, size_y, size_z):
    channels = padded.shape[0]
    summed = jnp.zeros((kernel.shape[2], size_x, size_y, size_z), jnp.float32)
    for step_x in range(3):
        stacked = stack_taps(padded, step_x, size_x, size_y, size_z)
        kernel_rows = kernel[9 * step_x : 9 * step_x + 9].reshape(9 * channels, kernel.shape[2])
        summed = summed + jnp.einsum(
            "io,ixyz->oxyz", kernel_rows, stacked, preferred_element_type=jnp.float32
        )
    return summed


def kernel_grad(padded, grad_pre, size_x, size_y, size_z):
    channels = padded.shape[0]
    pieces = []
    for step_x in range(3):
        stacked = stack_taps(padded, step_x, size_x, size_y, size_z)
        product = jnp.einsum("ixyz,oxyz->io", stacked, grad_pre, preferred_element_type=jnp.float32)
        pieces.append(product.reshape(9, channels, grad_pre.shape[0]))
    return jnp.concatenate(pieces, axis=0)


def widen(field):
    rimmed = padded_2(field, (("gx", 1), ("gy", 2)), 1)
    return jnp.pad(rimmed, ((0, 0), (0, 0), (0, 0), (1, 1)))


def select_rows(match, rows):
    shaped = match.reshape(match.shape + (1,) * (rows.ndim - 1))
    return jnp.sum(jnp.where(shaped, rows[None], jnp.zeros((), rows.dtype)), axis=1)


def local(
    point_feats,
    point_offsets,
    base_cells,
    block_owners,
    point_counts,
    lift_weight,
    conv_weight,
    read_weight,
    cotangent,
):
    local_blocks, channels, block_len = point_feats.shape
    slabs = lax.axis_size("gx")
    per_owner = max(2, (2 * local_blocks + slabs - 1) // slabs)
    slot_count = slabs * per_owner
    owners = block_owners[:, 0]
    order_ids = jnp.arange(local_blocks, dtype=jnp.int32)
    earlier = (owners[None, :] == owners[:, None]) & (order_ids[None, :] < order_ids[:, None])
    slot_of = owners * per_owner + jnp.sum(earlier.astype(jnp.int32), axis=1)
    slot_match = jnp.arange(slot_count, dtype=jnp.int32)[:, None] == slot_of[None, :]
    block_match = jnp.transpose(slot_match)
    positions = order_ids[:, None] * block_len + jnp.arange(block_len, dtype=jnp.int32)[None, :]
    alive_pts = positions < point_counts[0]
    masked = jnp.where(alive_pts[:, None, :], point_feats, jnp.zeros_like(point_feats))

    def place(rows):
        return select_rows(slot_match, rows)

    def take_home(rows):
        return select_rows(block_match, rows)

    arrived, arrived_offsets, arrived_base = (
        lax.all_to_all(place(masked), "gx", split_axis=0, concat_axis=0, tiled=True),
        lax.all_to_all(place(point_offsets), "gx", split_axis=0, concat_axis=0, tiled=True),
        lax.all_to_all(place(base_cells), "gx", split_axis=0, concat_axis=0, tiled=True),
    )
    lifted = jnp.einsum(
        "io,bip->bop", lift_weight, arrived, preferred_element_type=jnp.float32
    ).astype(jnp.bfloat16)
    factors = point_factors(arrived_offsets, arrived_base, CX, CY, NZ)
    latent = spread_dense(lifted.astype(jnp.float32), factors, NZ).astype(jnp.bfloat16)
    latent = latent.reshape(channels, CX, CY, NZ)
    latent_pad = widen(latent)
    pre_act = convolve(latent_pad, conv_weight, CX, CY, NZ)
    activated, gelu_back = jax.vjp(jax.nn.gelu, pre_act)
    latent_out = (latent.astype(jnp.float32) + activated).astype(jnp.bfloat16)
    sampled = sample_dense(latent_out.reshape(channels, CX * CY * NZ), factors, NZ).astype(
        jnp.bfloat16
    )
    grad_pred = jnp.where(alive_pts, cotangent, jnp.float32(0.0))
    returned = lax.all_to_all(sampled, "gx", split_axis=0, concat_axis=0, tiled=True)
    own_pred = jnp.einsum(
        "c,bcp->bp", read_weight, take_home(returned), preferred_element_type=jnp.float32
    )
    prediction = jnp.where(alive_pts, own_pred, jnp.float32(0.0))
    local_grad = (read_weight.astype(jnp.float32)[None, :, None] * grad_pred[:, None, :]).astype(
        jnp.bfloat16
    )
    grad_sampled = lax.all_to_all(place(local_grad), "gx", split_axis=0, concat_axis=0, tiled=True)
    grad_out = spread_dense(grad_sampled.astype(jnp.float32), factors, NZ)
    grad_out = grad_out.reshape(channels, CX, CY, NZ)
    grad_pre = gelu_back(grad_out)[0].astype(jnp.bfloat16)
    grad_pad = widen(grad_pre)
    flipped = jnp.transpose(conv_weight[::-1], (0, 2, 1))
    grad_latent = grad_out + convolve(grad_pad, flipped, CX, CY, NZ)
    kernel_part = kernel_grad(latent_pad, grad_pre, CX, CY, NZ)
    grad_conv = lax.psum(kernel_part, ("gx", "gy")) / slabs
    grad_lifted = sample_dense(grad_latent.reshape(channels, CX * CY * NZ), factors, NZ).astype(
        jnp.bfloat16
    )
    outgoing = jnp.einsum(
        "io,bop->bip", lift_weight, grad_lifted, preferred_element_type=jnp.float32
    ).astype(jnp.bfloat16)
    came_back = take_home(lax.all_to_all(outgoing, "gx", split_axis=0, concat_axis=0, tiled=True))
    grad_feats = jnp.where(alive_pts[:, None, :], came_back, jnp.zeros_like(came_back))
    return (prediction, grad_feats, grad_conv)


def solution(mesh):
    in_specs = (
        P(("gx", "gy"), None, None),
        P(("gx", "gy"), None, None),
        P(("gx", "gy"), None),
        P(("gx", "gy"), None),
        P(("gx", "gy")),
        P(),
        P(),
        P(),
        P(("gx", "gy"), None),
    )
    out_specs = (P(("gx", "gy"), None), P(("gx", "gy"), None, None), P())
    return jax.shard_map(local, mesh=mesh, in_specs=in_specs, out_specs=out_specs, check_vma=False)
```

profile of v0, /device:TPU:1, one launch (start us, length us, event | category | flops | bytes accessed | tf_op | source)
XLA Modules:
  0.0 510.9 jit_solution(16348951178917182916)
XLA Ops:
  10.5 9.4 %all-to-all-start = ((s32[32,2,128]{2,1,0:T(2,128)}), s32[32,2,128]{2,1,0:T(2,128)S(1)}, u32[]{:S(2)}, u32[]{:S(2)}) async-start(s32[32,2,128]{2,1,0:T(2,128)} %bitcast.33), calls=%async_computation | async-start | bytes 65536 | tf_op jit(solution)/shard_map/all_to_all | solution.py:217
  24.2 10.6 %select_reduce_fusion.1 = (bf16[64,32,128]{2,1,0:T(8,128)(2,1)}, bf16[64,32,128]{2,1,0:T(8,128)(2,1)}) fusion(pred[64,32]{1,0:T(8,128)(4,1)S(1)} %iota_compare_fusion.22, bf16[32,32,128]{2,1,0:T(8,128)(2,1)S(1)} %multiply_convert_fusion, bf16[32,32,128]{2,1,0:T(8,128)(2,1)S(1)} %broadcast_select_fusion.1), kind=kLoop, calls=%fused_computation.93 | loop fusion | flops 33030144 | bytes 1574912 | tf_op jit(solution)/shard_map/reduce_sum | solution.py:180
  38.5 7.4 %all-to-all-start.1 = ((bf16[64,3,128]{2,1,0:T(4,128)(2,1)}), bf16[64,3,128]{2,1,0:T(4,128)(2,1)S(1)}, u32[]{:S(2)}, u32[]{:S(2)}) async-start(bf16[64,3,128]{2,1,0:T(4,128)(2,1)} %select_reduce_fusion.4), calls=%async_computation.1 | async-start | bytes 131072 | tf_op jit(solution)/shard_map/all_to_all | solution.py:216
  46.2 7.0 %all-to-all-done.1 = bf16[64,3,128]{2,1,0:T(4,128)(2,1)S(1)} async-done(((bf16[64,3,128]{2,1,0:T(4,128)(2,1)}), bf16[64,3,128]{2,1,0:T(4,128)(2,1)S(1)}, u32[]{:S(2)}, u32[]{:S(2)}) %all-to-all-start.1) | async-done | bytes 49184 | tf_op jit(solution)/shard_map/all_to_all | solution.py:216
  53.3 3.9 all-to-all-start.2
  58.2 10.8 %all-to-all-done.2 = bf16[64,32,128]{2,1,0:T(8,128)(2,1)S(1)} async-done(((bf16[64,32,128]{2,1,0:T(8,128)(2,1)}), bf16[64,32,128]{2,1,0:T(8,128)(2,1)S(1)}, u32[]{:S(2)}, u32[]{:S(2)}) %all-to-all-start.2) | async-done | bytes 524320 | tf_op jit(solution)/shard_map/all_to_all | solution.py:215
  68.9 4.4 all-to-all-start.4
  74.7 68.9 %while.44 = (s32[]{:T(128)}, f32[512,256]{1,0:T(8,128)}, f32[8,8,128,16]{2,3,1,0:T(8,128)S(1)}, f32[8,8,32,128]{3,2,1,0:T(8,128)}, f32[8,8,128]{2,1,0:T(8,128)},...) while((s32[]{:T(128)}, f32[512,256]{1,0:T(8,128)}, ...), condition=%wide.region_5.6_spmd.clone, body=%wide.region_4.5_spmd.clone.sunk | while | flops 1081213952 | bytes 26202260 | solution.py:96
  86.9 2.4 fusion.171
  95.5 2.4 fusion.171
  129.9 2.4 fusion.171
  144.8 3.1 collective-permute-start
  155.6 3.8 collective-permute-start.2
  160.9 74.1 %while.45 = (s32[]{:T(128)}, f32[512,256]{1,0:T(8,128)}, f32[8,8,128,16]{2,3,1,0:T(8,128)S(1)}, f32[8,8,32,128]{3,2,1,0:T(8,128)}, f32[8,8,128]{2,1,0:T(8,128)},...) while((s32[]{:T(128)}, f32[512,256]{1,0:T(8,128)}, ...), condition=%wide.region_11.12_spmd.clone, body=%wide.region_10.11_spmd.clone.sunk | while | flops 1081213952 | bytes 26202260 | solution.py:96
  183.6 2.4 fusion.176
  230.0 2.4 fusion.176
  249.0 26.1 %while.42 = (s32[]{:T(128)}, bf16[8,8,32,128]{3,2,1,0:T(8,128)(2,1)}, f32[8,8,128,16]{2,3,1,0:T(8,128)S(1)}, s32[8,8,128]{2,1,0:T(8,128)}, bf16[32,16,256]{2,0,1...) while((s32[]{:T(128)}, bf16[8,8,32,128]{3,2,1,0:T(8,128)(2,1)}, ...), condition=%wide.region_7.8_spmd, body=%wide.region_6.7_spmd.sunk | while | flops 539984896 | bytes 5157473 | solution.py:136
  275.2 2.6 fusion.99
  277.8 4.0 collective-permute-start.6
  283.9 9.6 %all-to-all-start.3 = ((bf16[64,32,128]{2,1,0:T(8,128)(2,1)}), bf16[64,32,128]{2,1,0:T(8,128)(2,1)S(1)}, u32[]{:S(2)}, u32[]{:S(2)}) async-start(bf16[64,32,128]{2,1,0:T(8,128)(2,1)} %bitcast.55), calls=%async_computation.3 | async-start | bytes 1048576 | tf_op jit(solution)/shard_map/all_to_all | solution.py:233
  298.5 32.0 %while.43 = (s32[]{:T(128)}, bf16[8,8,32,128]{3,2,1,0:T(8,128)(2,1)S(1)}, f32[8,8,128,16]{2,3,1,0:T(8,128)S(1)}, s32[8,8,128]{2,1,0:T(8,128)}, bf16[32,16,256]{2...) while((s32[]{:T(128)}, ...), condition=%wide.region_13.14_spmd, body=%wide.region_12.13_spmd.sunk | while | flops 1078428672 | bytes 14078061 | solution.py:136
  331.6 7.5 %all-to-all-start.5 = ((bf16[64,32,128]{2,1,0:T(8,128)(2,1)}), bf16[64,32,128]{2,1,0:T(8,128)(2,1)S(1)}, u32[]{:S(2)}, u32[]{:S(2)}) async-start(bf16[64,32,128]{2,1,0:T(8,128)(2,1)} %fusion.54), calls=%async_computation.5 | async-start | bytes 1048576 | tf_op jit(solution)/shard_map/all_to_all | solution.py:256
  340.2 150.0 %all-reduce.4.cloned.1.call-done = f32[27,32,32]{2,1,0:T(8,128)} async-done(((f32[27,32,32]{2,1,0:T(8,128)}), f32[27,32,32]{2,1,0:T(8,128)}) %all-reduce.4.cloned.1.call-update) | async-done | bytes 110608 | tf_op jit(solution)/shard_map/psum | solution.py:249
  491.9 10.5 %select_reduce_fusion = (bf16[32,32,128]{2,1,0:T(8,128)(2,1)S(1)}, bf16[32,32,128]{2,1,0:T(8,128)(2,1)S(1)}) fusion(pred[32,64]{1,0:T(8,128)(4,1)S(1)} %iota_compare_fusion.24, bf16[64,32,128]{2,1,0:T(8,128)(2,1)S(1)} %all-to-all-done.5, bf16[64,32,128]{2,1,0:T(8,128)(2,1)S(1)} %all-to-all-done.3), kind=kLoop, calls=%fused_computation.92 | loop fusion | flops 33292288 | bytes 1574912 | tf_op jit(solution)/shard_map/reduce_sum | solution.py:180
  (462 shorter events, 237.3 us)
Async XLA Ops:
  7.2 66.2 %copy-start = (bf16[32,32]{1,0:T(8,128)(2,1)S(1)}, bf16[32,32]{1,0:T(8,128)(2,1)}, u32[]{:S(2)}) copy-start(bf16[32,32]{1,0:T(8,128)(2,1)} %param.22) | copy-start | bytes 6148
  7.2 27.7 %copy-start.21 = (bf16[32,3,128]{2,0,1:T(8,128)(2,1)S(1)}, bf16[32,3,128]{2,0,1:T(8,128)(2,1)}, u32[]{:S(2)}) copy-start(bf16[32,3,128]{2,0,1:T(8,128)(2,1)} %param.18) | copy-start | bytes 73732
  8.8 14.5 %copy-start.24 = (s32[32]{0:T(128)}, s32[32]{0:T(128)S(1)}, u32[]{:S(2)}) copy-start(s32[32]{0:T(128)S(1)} %multiply_add_fusion) | copy-start | bytes 388
  10.5 28.0 %all-to-all-start = ((s32[32,2,128]{2,1,0:T(2,128)}), s32[32,2,128]{2,1,0:T(2,128)S(1)}, u32[]{:S(2)}, u32[]{:S(2)}) async-start(s32[32,2,128]{2,1,0:T(2,128)} %bitcast.33), calls=%async_computation | async-start | bytes 65536 | tf_op jit(solution)/shard_map/all_to_all | solution.py:217
  38.5 14.8 %all-to-all-start.1 = ((bf16[64,3,128]{2,1,0:T(4,128)(2,1)}), bf16[64,3,128]{2,1,0:T(4,128)(2,1)S(1)}, u32[]{:S(2)}, u32[]{:S(2)}) async-start(bf16[64,3,128]{2,1,0:T(4,128)(2,1)} %select_reduce_fusion.4), calls=%async_computation.1 | async-start | bytes 131072 | tf_op jit(solution)/shard_map/all_to_all | solution.py:216
  53.3 15.7 %all-to-all-start.2 = ((bf16[64,32,128]{2,1,0:T(8,128)(2,1)}), bf16[64,32,128]{2,1,0:T(8,128)(2,1)S(1)}, u32[]{:S(2)}, u32[]{:S(2)}) async-start(bf16[64,32,128]{2,1,0:T(8,128)(2,1)} %get-tuple-element.223), calls=%async_computation.2 | async-start | bytes 1048576 | tf_op jit(solution)/shard_map/all_to_all | solution.py:215
  68.9 81.6 %all-to-all-start.4 = ((bf16[64,32,128]{2,1,0:T(8,128)(2,1)}), bf16[64,32,128]{2,1,0:T(8,128)(2,1)}, u32[]{:S(2)}, u32[]{:S(2)}) async-start(bf16[64,32,128]{2,1,0:T(8,128)(2,1)} %get-tuple-element.222), calls=%async_computation.4 | async-start | bytes 1048576 | tf_op jit(solution)/shard_map/all_to_all | solution.py:241
  74.7 73.2 %copy-start.6 = (bf16[27,32,32]{2,1,0:T(8,128)(2,1)S(1)}, bf16[27,32,32]{2,1,0:T(8,128)(2,1)}, u32[]{:S(2)}) copy-start(bf16[27,32,32]{2,1,0:T(8,128)(2,1)} %param.23) | copy-start | bytes 165892
  143.6 9.1 %copy-start.10 = (s32[8,8,128]{2,1,0:T(8,128)}, s32[8,8,128]{2,1,0:T(8,128)S(1)}, u32[]{:S(2)}) copy-start(s32[8,8,128]{2,1,0:T(8,128)S(1)} %get-tuple-element.731) | copy-start | bytes 98308
  144.8 7.9 %collective-permute-start = (bf16[32,1,8,256]{3,0,2,1:T(8,128)(2,1)S(1)}, bf16[32,1,8,256]{3,0,2,1:T(8,128)(2,1)S(1)}, u32[]{:S(2)}, u32[]{:S(2)}) collective-permute-start(bf16[32,1,8,256]{3,0,2,1:T(8,128)(2,1)S(1)} %get-tuple-element.372), channel_id=1, source_target_pairs={{0,4},{4,8},{8,12},{12,16},{16,20},{20,24},{24,28},{28,32},{32,36}... | collective-permute-start | bytes 393224 | tf_op jit(solution)/shard_map/ppermute | solution.py:24
  148.6 6.3 %collective-permute-start.1 = (bf16[32,1,8,256]{3,0,2,1:T(8,128)(2,1)S(1)}, bf16[32,1,8,256]{3,0,2,1:T(8,128)(2,1)S(1)}, u32[]{:S(2)}, u32[]{:S(2)}) collective-permute-start(bf16[32,1,8,256]{3,0,2,1:T(8,128)(2,1)S(1)} %get-tuple-element.371), channel_id=1, source_target_pairs={{4,0},{8,4},{12,8},{16,12},{20,16},{24,20},{28,24},{32,28},{36,32}... | collective-permute-start | bytes 393224 | tf_op jit(solution)/shard_map/ppermute | solution.py:26
  155.6 79.4 %collective-permute-start.2 = (bf16[32,4,1,256]{3,0,2,1:T(8,128)(2,1)}, bf16[32,4,1,256]{3,0,2,1:T(8,128)(2,1)}, u32[]{:S(2)}, u32[]{:S(2)}) collective-permute-start(bf16[32,4,1,256]{3,0,2,1:T(8,128)(2,1)} %get-tuple-element.362), channel_id=1, source_target_pairs={{0,1},{1,2},{2,3},{4,5},{5,6},{6,7},{8,9},{9,10},{10,11},{12,13},{... | collective-permute-start | bytes 196616 | tf_op jit(solution)/shard_map/ppermute | solution.py:24
  159.4 75.6 %collective-permute-start.3 = (bf16[32,4,1,256]{3,0,2,1:T(8,128)(2,1)}, bf16[32,4,1,256]{3,0,2,1:T(8,128)(2,1)}, u32[]{:S(2)}, u32[]{:S(2)}) collective-permute-start(bf16[32,4,1,256]{3,0,2,1:T(8,128)(2,1)} %get-tuple-element.363), channel_id=1, source_target_pairs={{1,0},{2,1},{3,2},{5,4},{6,5},{7,6},{9,8},{10,9},{11,10},{13,12},{... | collective-permute-start | bytes 196616 | tf_op jit(solution)/shard_map/ppermute | solution.py:26
  243.8 33.9 %collective-permute-start.4 = (bf16[32,1,8,256]{3,0,2,1:T(8,128)(2,1)S(1)}, bf16[32,1,8,256]{3,0,2,1:T(8,128)(2,1)S(1)}, u32[]{:S(2)}, u32[]{:S(2)}) collective-permute-start(bf16[32,1,8,256]{3,0,2,1:T(8,128)(2,1)S(1)} %get-tuple-element.367), channel_id=1, source_target_pairs={{0,4},{4,8},{8,12},{12,16},{16,20},{20,24},{24,28},{28,32},{32,36}... | collective-permute-start | bytes 393224 | tf_op jit(solution)/shard_map/ppermute | solution.py:24
  245.9 31.9 %collective-permute-start.5 = (bf16[32,1,8,256]{3,0,2,1:T(8,128)(2,1)S(1)}, bf16[32,1,8,256]{3,0,2,1:T(8,128)(2,1)S(1)}, u32[]{:S(2)}, u32[]{:S(2)}) collective-permute-start(bf16[32,1,8,256]{3,0,2,1:T(8,128)(2,1)S(1)} %get-tuple-element.368), channel_id=1, source_target_pairs={{4,0},{8,4},{12,8},{16,12},{20,16},{24,20},{28,24},{32,28},{36,32}... | collective-permute-start | bytes 393224 | tf_op jit(solution)/shard_map/ppermute | solution.py:26
  277.8 15.7 %collective-permute-start.6 = (bf16[32,4,1,256]{3,0,2,1:T(8,128)(2,1)S(1)}, bf16[32,4,1,256]{3,0,2,1:T(8,128)(2,1)S(1)}, u32[]{:S(2)}, u32[]{:S(2)}) collective-permute-start(bf16[32,4,1,256]{3,0,2,1:T(8,128)(2,1)S(1)} %get-tuple-element.360), channel_id=1, source_target_pairs={{0,1},{1,2},{2,3},{4,5},{5,6},{6,7},{8,9},{9,10},{10,11},{12,13},{... | collective-permute-start | bytes 196616 | tf_op jit(solution)/shard_map/ppermute | solution.py:24
  281.8 11.7 %collective-permute-start.7 = (bf16[32,4,1,256]{3,0,2,1:T(8,128)(2,1)S(1)}, bf16[32,4,1,256]{3,0,2,1:T(8,128)(2,1)S(1)}, u32[]{:S(2)}, u32[]{:S(2)}) collective-permute-start(bf16[32,4,1,256]{3,0,2,1:T(8,128)(2,1)S(1)} %get-tuple-element.361), channel_id=1, source_target_pairs={{1,0},{2,1},{3,2},{5,4},{6,5},{7,6},{9,8},{10,9},{11,10},{13,12},{... | collective-permute-start | bytes 196616 | tf_op jit(solution)/shard_map/ppermute | solution.py:26
  283.9 47.8 %all-to-all-start.3 = ((bf16[64,32,128]{2,1,0:T(8,128)(2,1)}), bf16[64,32,128]{2,1,0:T(8,128)(2,1)S(1)}, u32[]{:S(2)}, u32[]{:S(2)}) async-start(bf16[64,32,128]{2,1,0:T(8,128)(2,1)} %bitcast.55), calls=%async_computation.3 | async-start | bytes 1048576 | tf_op jit(solution)/shard_map/all_to_all | solution.py:233
  330.5 9.5 %copy-start.25 = (s32[32]{0:T(128)S(1)}, s32[32]{0:T(128)}, u32[]{:S(2)}) copy-start(s32[32]{0:T(128)} %copy-done.24) | copy-start | bytes 388
  331.6 170.8 %copy-start.18 = (pred[32,128]{1,0:T(8,128)(4,1)S(1)}, pred[32,128]{1,0:T(8,128)(4,1)}, u32[]{:S(2)}) copy-start(pred[32,128]{1,0:T(8,128)(4,1)} %copy-done.17) | copy-start | bytes 12292
  331.6 160.3 %all-to-all-start.5 = ((bf16[64,32,128]{2,1,0:T(8,128)(2,1)}), bf16[64,32,128]{2,1,0:T(8,128)(2,1)S(1)}, u32[]{:S(2)}, u32[]{:S(2)}) async-start(bf16[64,32,128]{2,1,0:T(8,128)(2,1)} %fusion.54), calls=%async_computation.5 | async-start | bytes 1048576 | tf_op jit(solution)/shard_map/all_to_all | solution.py:256
  339.2 164.0 %copy-start.26 = (bf16[32]{0:T(256)(128)(2,1)S(1)}, bf16[32]{0:T(256)(128)(2,1)}, u32[]{:S(2)}) copy-start(bf16[32]{0:T(256)(128)(2,1)} %param.24) | copy-start | bytes 196
  339.2 164.1 %copy-start.23 = (s32[32]{0:T(128)S(1)}, s32[32]{0:T(128)}, u32[]{:S(2)}) copy-start(s32[32]{0:T(128)} %copy-done.22) | copy-start | bytes 388
  339.2 150.9 %all-reduce.4.cloned.1.call-start = ((), (), s32[]{:S(2)}) async-start(), calls=%async_computation.6 | async-start | bytes 884736 | tf_op jit(solution)/shard_map/psum | solution.py:249
  (32 other events, 89.0 us)
Sparse Core Ops, SparseCore 0:
  345.4 144.6 all-reduce.3
where the time goes:
time: 515 us; the launch traced here: 511 us
  waiting for transfers between devices  170 us (33%)
  matrix products  120 us (23%)
  other arithmetic  87.2 us (17%)
  starting transfers between devices  62.3 us (12%)
  local copies, waits for them, and re-layouts  54.2 us (11%)
  between operations  15.5 us (3%)
    psum x1, waiting for transfers between devices, local(): grad_conv = lax.psum(kernel_part, ('gx', 'gy')) / slabs  150 us
    dot_general x32, matrix products, add_group(): total = total + jnp.dot(high, right, preferred_element_type=jnp.float32)  47.6 us
    dot_general x32, matrix products, add_group(): total = total + jnp.dot(low, right, preferred_element_type=jnp.float32)  31.7 us
    mul x16, other arithmetic, add_group(): based * factor[None, None]  29.6 us
    reduce_sum x4, other arithmetic, select_rows(): jnp.sum(jnp.where(shaped, rows[None], jnp.zeros((), rows.dtype)), axis=1)  24.3 us
    dot_general x24, matrix products, read_group(): jnp.einsum('ckd,sbd->cksb', part, upper, preferred_element_type=jnp.float32)  16.9 us
    squeeze x80, local copies, waits for them, and re-layouts, spread_dense(): lax.scan(add_group, start, (vals_g, plane_g, near_g, far_g, level_g))  16.6 us
    add x32, other arithmetic, level_onehots(): upper = (levels == corner_c[:, :, None] + 1).astype(jnp.bfloat16)  16.3 us
  transfers between devices with their start and end apart: 15, of which 4 were waited for; matrix products, arithmetic and copies ran while one was open for 46% of the time, Pallas kernels for 0%

commit v1 on v0

v1 whole, which is shorter than its diff:
```python
import functools

import jax
import jax.numpy as jnp
from jax import lax
from jax.experimental import pallas as pl
from jax.experimental.pallas import tpu as pltpu
from jax.sharding import PartitionSpec as P

C = 32
CX = 2
CY = 8
NZ = 256
NB = 32
BLK = 128
GX = 32
GY = 4
CAP = 2
PTS = CAP * BLK
COLS = CX * CY
TAPS = 27
MESH = pl.DeviceIdType.MESH
BF = jnp.bfloat16
F32 = jnp.float32


def dot(a, b, ca=1, cb=0):
    return lax.dot_general(a, b, (((ca,), (cb,)), ((), ())), preferred_element_type=F32)


def slots_kernel(owners, inv, slot, cnt):
    @pl.loop(0, GX)
    def _(o):
        cnt[o] = 0
        inv[CAP * o] = -1
        inv[CAP * o + 1] = -1

    @pl.loop(0, NB)
    def _(j):
        o = owners[j, 0]
        r = cnt[o]
        cnt[o] = r + 1
        s = CAP * o + r
        inv[s] = j
        slot[j] = s


def slot_tables(owners):
    smem = pl.BlockSpec(memory_space=pltpu.SMEM)
    return pl.pallas_call(
        slots_kernel,
        out_shape=(
            jax.ShapeDtypeStruct((GX * CAP,), jnp.int32),
            jax.ShapeDtypeStruct((NB,), jnp.int32),
        ),
        in_specs=[smem],
        out_specs=(smem, smem),
        scratch_shapes=[pltpu.SMEM((GX,), jnp.int32)],
    )(owners)


def shifted(values, step):
    lanes = lax.broadcasted_iota(jnp.int32, values.shape, 1)
    if step == 1:
        return jnp.where(lanes == 0, 0.0, pltpu.roll(values, 1, 1))
    return jnp.where(lanes == NZ - 1, 0.0, pltpu.roll(values, NZ - 1, 1))


def conv_pair(weights, padded, pair):
    window = padded[2 * pair : 2 * pair + 4].reshape(4 * 4 * C, NZ)
    part = dot(weights[...], window)
    return shifted(part[0:128], 1) + part[128:256] + shifted(part[256:384], -1)


def kernel(
    inv, slot, count, feats, offsets, base, cot, lift, conv, read,
    pred_out, feats_out, conv_out,
    bmat, cmat, ghi, glo, send, recv, acc, zs, planes, latp, gp, gs, wf, wb,
    gout, field, gl, predmsg, predr, gfs, gfr, redsrc, red1, red2, red3,
    s_send, s_recv, h_send, h_recv, i_send, i_recv, p_send, p_recv,
    f_send, f_recv, a_send, a_recv, b_send, b_recv, c_send, c_recv,
):
    mx = lax.axis_index("gx")
    my = lax.axis_index("gy")
    right, left = lax.rem(mx + 1, GX), lax.rem(mx + GX - 1, GX)
    up, down = lax.rem(my + 1, GY), lax.rem(my + GY - 1, GY)

    barrier = pltpu.get_barrier_semaphore()

    @pl.loop(1, GX)
    def _(k):
        pl.semaphore_signal(barrier, inc=1, device_id=(lax.rem(mx + k, GX), my), device_id_type=MESH)

    for k in range(1, GY):
        pl.semaphore_signal(barrier, inc=1, device_id=(mx, lax.rem(my + k, GY)), device_id_type=MESH)
    for px in (left, right):
        for py in (down, up):
            pl.semaphore_signal(barrier, inc=1, device_id=(px, py), device_id_type=MESH)

    cells = base[...].astype(F32)
    rows_b = jnp.floor((cells + 0.5) * (1.0 / (NZ - 1)))
    bmat[...] = rows_b
    cmat[...] = cells - rows_b * (NZ - 1.0)
    live_count = count[0]
    position = lax.broadcasted_iota(jnp.int32, (NB, BLK), 0) * BLK + lax.broadcasted_iota(
        jnp.int32, (NB, BLK), 1
    )
    grad = jnp.where(position < live_count, cot[...], 0.0)
    high = grad.astype(BF).astype(F32)
    ghi[...] = high
    glo[...] = grad - high
    lane32 = lax.broadcasted_iota(jnp.int32, (C, BLK), 1)
    sub8 = lax.broadcasted_iota(jnp.int32, (8, BLK), 0)

    def place(o):
        tails = []
        for r in range(CAP):
            j = inv[CAP * o + r]
            jj = jnp.maximum(j, 0)
            live = jnp.where(j >= 0, live_count - jj * BLK, 0)
            block = jnp.where(lane32 < live, feats[jj].astype(F32), 0.0)
            send[o, r * C : (r + 1) * C, :] = block.astype(BF)
            off = offsets[jj].astype(F32)
            here = jnp.where(j >= 0, 1.0, 0.0)
            tail = jnp.where(sub8 == 0, off[0:1], 0.0)
            tail = jnp.where(sub8 == 1, off[1:2], tail)
            tail = jnp.where(sub8 == 2, off[2:3], tail)
            tail = jnp.where(sub8 == 3, bmat[pl.ds(jj, 1), :], tail)
            tail = jnp.where(sub8 == 4, cmat[pl.ds(jj, 1), :], tail)
            tail = jnp.where(sub8 == 5, ghi[pl.ds(jj, 1), :] * here, tail)
            tail = jnp.where(sub8 == 6, glo[pl.ds(jj, 1), :] * here, tail)
            tails.append(tail)
        send[o, CAP * C : CAP * C + 16, :] = jnp.concatenate(tails, axis=0).astype(BF)

    @pl.loop(0, GX)
    def _(o):
        place(o)

    pl.semaphore_wait(barrier, GX - 1 + GY - 1 + 4)

    def points_copy(k):
        to = lax.rem(mx + k, GX)
        return pltpu.make_async_remote_copy(
            src_ref=send.at[to], dst_ref=recv.at[mx],
            send_sem=s_send.at[k], recv_sem=s_recv.at[k],
            device_id=(to, my), device_id_type=MESH,
        )

    @pl.loop(1, GX)
    def _(k):
        points_copy(k).start()

    def place_tap(xp):
        lanes = lax.broadcasted_iota(jnp.int32, (C, 128), 1)
        rows = lax.broadcasted_iota(jnp.int32, (C, 128), 0)
        return jnp.where(lanes == rows + C * xp, 1.0, 0.0).astype(BF)

    spots = [place_tap(xp) for xp in range(4)]
    wf[...] = jnp.zeros(wf.shape, BF)
    wb[...] = jnp.zeros(wb.shape, BF)
    for dz in range(3):
        for dy in range(3):
            for xo in range(2):
                tile_f = sum(
                    dot(conv[9 * dx + 3 * dy + dz], spots[dx + xo], 0, 0) for dx in range(3)
                ).astype(BF)
                tile_b = sum(
                    dot(conv[9 * (2 - dx) + 3 * (2 - dy) + (2 - dz)], spots[dx + xo])
                    for dx in range(3)
                ).astype(BF)
                for yo in range(2):
                    row = ((dz * 2 + yo) * 2 + xo) * C
                    lane = (yo + dy) * 128
                    wf[row : row + C, lane : lane + 128] = tile_f
                    wb[row : row + C, lane : lane + 128] = tile_b
    eye = jnp.where(
        lax.broadcasted_iota(jnp.int32, (C, C), 0) == lax.broadcasted_iota(jnp.int32, (C, C), 1),
        1.0, 0.0,
    )
    read_col = dot((eye * read[...].astype(F32)).astype(BF), jnp.ones((C, NZ), BF))
    lift_w = lift[...]

    sub_z = lax.broadcasted_iota(jnp.int32, (NZ, PTS), 0).astype(F32)
    sub_y = lax.broadcasted_iota(jnp.int32, (CY, PTS), 0).astype(F32)

    def spread(msg, k):
        block = jnp.concatenate([msg[0:C], msg[C : 2 * C]], axis=1)
        tail = msg[2 * C : 2 * C + 16].astype(F32)
        tail = jnp.concatenate([tail[0:8], tail[8:16]], axis=1)
        near = jnp.exp(-2.0 * tail * tail)
        far = jnp.exp(-2.0 * (tail - 1.0) * (tail - 1.0))
        at_y, at_z = tail[3:4], tail[4:5]
        slope = tail[5:6] + tail[6:7]
        wy = jnp.where(sub_y == at_y, near[1:2], jnp.where(sub_y == at_y + 1.0, far[1:2], 0.0))
        plane = (near[0:1] * wy, far[0:1] * wy)
        planes[k, 0:CY, :] = plane[0]
        planes[k, CY : 2 * CY, :] = plane[1]
        z = jnp.where(sub_z == at_z, near[2:3], jnp.where(sub_z == at_z + 1.0, far[2:3], 0.0))
        z = z.astype(BF)
        zs[k] = z
        lifted = dot(lift_w, block, 0, 0).astype(BF).astype(F32)
        rows = [
            (lifted * plane[x][y : y + 1]).astype(BF) for y in range(CY) for x in range(CX)
        ]
        rows.append(jnp.concatenate([plane[0] * slope, plane[1] * slope], axis=0).astype(BF))
        return dot(jnp.concatenate(rows, axis=0), z, 1, 1)

    acc[...] = spread(send[mx], 0)

    @pl.loop(1, GX)
    def _(k):
        points_copy(k).wait_recv()
        acc[...] += spread(recv[lax.rem(mx - k + GX, GX)], k)

    def halo_copies(buf, sends, recvs):
        ends = (
            (right, my, buf.at[1:9, 2], buf.at[1:9, 0]),
            (left, my, buf.at[1:9, 1], buf.at[1:9, 3]),
            (mx, up, buf.at[8, 1:3], buf.at[0, 1:3]),
            (mx, down, buf.at[1, 1:3], buf.at[9, 1:3]),
            (right, up, buf.at[8, 2], buf.at[0, 0]),
            (right, down, buf.at[1, 2], buf.at[9, 0]),
            (left, up, buf.at[8, 1], buf.at[0, 3]),
            (left, down, buf.at[1, 1], buf.at[9, 3]),
        )
        return [
            pltpu.make_async_remote_copy(
                src_ref=src, dst_ref=dst, send_sem=sends.at[n], recv_sem=recvs.at[n],
                device_id=(px, py), device_id_type=MESH,
            )
            for n, (px, py, src, dst) in enumerate(ends)
        ]

    def clear_ends(buf):
        @pl.when(mx == 0)
        def _():
            buf[:, 0] = jnp.zeros((10, C, NZ), BF)

        @pl.when(mx == GX - 1)
        def _():
            buf[:, 3] = jnp.zeros((10, C, NZ), BF)

        @pl.when(my == 0)
        def _():
            buf[0] = jnp.zeros((4, C, NZ), BF)

        @pl.when(my == GY - 1)
        def _():
            buf[9] = jnp.zeros((4, C, NZ), BF)

    for y in range(CY):
        for x in range(CX):
            row = (y * CX + x) * C
            latp[y + 1, x + 1] = acc[row : row + C, :].astype(BF)
    halos = halo_copies(latp, h_send, h_recv)
    for copy in halos:
        copy.start()
    for copy in halos:
        copy.wait_recv()
    for copy in halos:
        copy.wait_send()
    clear_ends(latp)

    for pair in range(4):
        pre = conv_pair(wf, latp, pair)
        cube = pre * pre
        th = jnp.tanh(0.7978845608028654 * pre * (1.0 + 0.044715 * cube))
        half = 0.5 * (1.0 + th)
        slope = half + 0.5 * pre * (1.0 - th * th) * (
            0.7978845608028654 * (1.0 + 3.0 * 0.044715 * cube)
        )
        own = latp[2 * pair + 1 : 2 * pair + 3, 1:3].reshape(4 * C, NZ).astype(F32)
        out = (own + pre * half).astype(BF).astype(F32)
        grads = []
        for yo in range(2):
            for x in range(CX):
                row = x * CY + 2 * pair + yo
                n = (yo * CX + x) * C
                field[row : row + 1, :] = jnp.sum(
                    out[n : n + C] * read_col, axis=0, keepdims=True
                )
                grads.append(read_col * acc[COLS * C + row : COLS * C + row + 1, :])
        grad_out = jnp.concatenate(grads, axis=0)
        gout[128 * pair : 128 * pair + 128, :] = grad_out
        grad_pre = (grad_out * slope).astype(BF)
        gp[2 * pair + 1 : 2 * pair + 3, 1:3] = grad_pre.reshape(2, 2, C, NZ)
        wide = grad_pre.astype(F32)
        gs[pair, 0:128, :] = shifted(wide, -1).astype(BF)
        gs[pair, 128:256, :] = grad_pre
        gs[pair, 256:384, :] = shifted(wide, 1).astype(BF)
    halos2 = halo_copies(gp, i_send, i_recv)
    for copy in halos2:
        copy.start()

    tap = jnp.zeros((4 * 4 * C, 3 * 128), F32)
    for pair in range(4):
        window = latp[2 * pair : 2 * pair + 4].reshape(4 * 4 * C, NZ)
        tap = tap + dot(window, gs[pair], 1, 1)
    quarter = lax.broadcasted_iota(jnp.int32, (C, 128), 1) // C
    quarter8 = lax.broadcasted_iota(jnp.int32, (8, 128), 1) // C
    for dx in range(3):
        for dy in range(3):
            for dz in range(3):
                total = jnp.zeros((C, 128), F32)
                for yo in range(2):
                    for xo in range(2):
                        n = ((yo + dy) * 4 + xo + dx) * C
                        piece = tap[n : n + C, dz * 128 : dz * 128 + 128]
                        total = jnp.where(quarter == 2 * yo + xo, piece, total)
                total = total + pltpu.roll(total, 64, 1)
                total = total + pltpu.roll(total, 32, 1)
                packed = total[0:8]
                for q in range(1, 4):
                    packed = jnp.where(quarter8 == q, total[8 * q : 8 * q + 8], packed)
                redsrc[9 * dx + 3 * dy + dz] = packed
    redsrc[TAPS:GX] = jnp.zeros((GX - TAPS, 8, 128), F32)

    def taps_copy(k):
        to = lax.rem(mx + k, GX)
        return pltpu.make_async_remote_copy(
            src_ref=redsrc.at[to], dst_ref=red1.at[mx],
            send_sem=a_send.at[k], recv_sem=a_recv.at[k],
            device_id=(to, my), device_id_type=MESH,
        )

    @pl.loop(1, GX)
    def _(k):
        taps_copy(k).start()

    scalar = field[...]
    scalar_hi = scalar.astype(BF)
    scalar_lo = (scalar - scalar_hi.astype(F32)).astype(BF)
    scalars = jnp.concatenate([scalar_hi, scalar_lo], axis=0)

    def read_points(k):
        got = dot(scalars, zs[k])
        total = jnp.sum((got[0:COLS] + got[COLS:]) * planes[k], axis=0, keepdims=True)
        return total[:, 0:BLK], total[:, BLK:]

    def pred_copy(k):
        to = lax.rem(mx - k + GX, GX)
        return pltpu.make_async_remote_copy(
            src_ref=predmsg.at[k], dst_ref=predr.at[mx],
            send_sem=p_send.at[k], recv_sem=p_recv.at[k],
            device_id=(to, my), device_id_type=MESH,
        )

    first, second = read_points(0)
    predr[mx, 0:1, :] = first
    predr[mx, 1:2, :] = second

    @pl.loop(1, GX)
    def _(k):
        one, two = read_points(k)
        predmsg[k, 0:1, :] = one
        predmsg[k, 1:2, :] = two
        predmsg[k, 2:8, :] = jnp.zeros((6, BLK), F32)
        pred_copy(k).start()

    for copy in halos2:
        copy.wait_recv()
    for copy in halos2:
        copy.wait_send()
    clear_ends(gp)
    for pair in range(4):
        back = conv_pair(wb, gp, pair)
        gl[128 * pair : 128 * pair + 128, :] = (
            gout[128 * pair : 128 * pair + 128, :] + back
        ).astype(BF)

    red1[mx] = redsrc[mx]

    @pl.loop(1, GX)
    def _(k):
        taps_copy(k).wait_recv()

    red2[my] = jnp.sum(red1[...], axis=0)

    def rows_copy(k):
        return pltpu.make_async_remote_copy(
            src_ref=red2.at[my], dst_ref=red2.at[my],
            send_sem=b_send.at[k], recv_sem=b_recv.at[k],
            device_id=(mx, lax.rem(my + k, GY)), device_id_type=MESH,
        )

    for k in range(1, GY):
        rows_copy(k).start()

    def gather(k):
        got = dot(gl[...], zs[k])
        total = jnp.zeros((C, PTS), F32)
        for y in range(CY):
            for x in range(CX):
                n = (y * CX + x) * C
                total = total + got[n : n + C] * planes[k, x * CY + y : x * CY + y + 1, :]
        back = dot(lift_w, total.astype(BF)).astype(BF)
        return back[:, 0:BLK], back[:, BLK:]

    def feats_copy(k):
        to = lax.rem(mx - k + GX, GX)
        return pltpu.make_async_remote_copy(
            src_ref=gfs.at[k], dst_ref=gfr.at[pl.ds(CAP * mx, CAP)],
            send_sem=f_send.at[k], recv_sem=f_recv.at[k],
            device_id=(to, my), device_id_type=MESH,
        )

    def send_back(k):
        one, two = gather(k)
        gfs[k, 0] = one
        gfs[k, 1] = two
        feats_copy(k).start()

    @pl.loop(1, 12)
    def _(k):
        send_back(k)

    for k in range(1, GY):
        rows_copy(k).wait_recv()
    for k in range(1, GY):
        rows_copy(k).wait_send()
    red3[mx] = (red2[0] + red2[1] + red2[2] + red2[3]) * (1.0 / GX)

    def total_copy(k):
        to = lax.rem(mx + k, GX)
        return pltpu.make_async_remote_copy(
            src_ref=red3.at[mx], dst_ref=red3.at[mx],
            send_sem=c_send.at[k], recv_sem=c_recv.at[k],
            device_id=(to, my), device_id_type=MESH,
        )

    @pl.loop(1, GX)
    def _(k):
        total_copy(k).start()

    @pl.loop(12, GX)
    def _(k):
        send_back(k)

    first_gf, second_gf = gather(0)
    gfr[CAP * mx] = first_gf
    gfr[CAP * mx + 1] = second_gf

    @pl.loop(1, GX)
    def _(k):
        pred_copy(k).wait_recv()
        total_copy(k).wait_recv()

    for d in range(TAPS):
        packed = red3[d]
        for q in range(4):
            piece = packed if q == 0 else pltpu.roll(packed, 128 - C * q, 1)
            conv_out[d, 8 * q : 8 * q + 8, :] = piece[:, 0:C]

    @pl.loop(1, GX)
    def _(k):
        feats_copy(k).wait_recv()

    lane1 = lax.broadcasted_iota(jnp.int32, (1, BLK), 1)

    @pl.loop(0, NB)
    def _(j):
        s = slot[j]
        live = live_count - j * BLK
        feats_out[j] = jnp.where(lane32 < live, gfr[s].astype(F32), 0.0).astype(BF)
        both = predr[s // CAP]
        value = jnp.where(lax.rem(s, CAP) == 0, both[0:1], both[1:2])
        pred_out[pl.ds(j, 1), :] = jnp.where(lane1 < live, value, 0.0)

    @pl.loop(1, GX)
    def _(k):
        points_copy(k).wait_send()
        taps_copy(k).wait_send()
        pred_copy(k).wait_send()
        feats_copy(k).wait_send()
        total_copy(k).wait_send()


def local(
    point_feats, point_offsets, base_cells, block_owners, point_counts,
    lift_weight, conv_weight, read_weight, cotangent,
):
    inv, slot = slot_tables(block_owners)
    smem = pl.BlockSpec(memory_space=pltpu.SMEM)
    vmem = pl.BlockSpec(memory_space=pltpu.VMEM)
    dma = pltpu.SemaphoreType.DMA
    return pl.pallas_call(
        kernel,
        out_shape=(
            jax.ShapeDtypeStruct((NB, BLK), F32),
            jax.ShapeDtypeStruct((NB, C, BLK), BF),
            jax.ShapeDtypeStruct((TAPS, C, C), F32),
        ),
        in_specs=[smem, smem, smem] + [vmem] * 7,
        out_specs=(vmem, vmem, vmem),
        scratch_shapes=[
            pltpu.VMEM((NB, BLK), F32),
            pltpu.VMEM((NB, BLK), F32),
            pltpu.VMEM((NB, BLK), F32),
            pltpu.VMEM((NB, BLK), F32),
            pltpu.VMEM((GX, CAP * C + 16, BLK), BF),
            pltpu.VMEM((GX, CAP * C + 16, BLK), BF),
            pltpu.VMEM((COLS * C + COLS, NZ), F32),
            pltpu.VMEM((GX, NZ, PTS), BF),
            pltpu.VMEM((GX, COLS, PTS), F32),
            pltpu.VMEM((10, 4, C, NZ), BF),
            pltpu.VMEM((10, 4, C, NZ), BF),
            pltpu.VMEM((4, 3 * 128, NZ), BF),
            pltpu.VMEM((3 * 128, 512), BF),
            pltpu.VMEM((3 * 128, 512), BF),
            pltpu.VMEM((COLS * C, NZ), F32),
            pltpu.VMEM((COLS, NZ), F32),
            pltpu.VMEM((COLS * C, NZ), BF),
            pltpu.VMEM((GX, 8, BLK), F32),
            pltpu.VMEM((GX, 8, BLK), F32),
            pltpu.VMEM((GX, CAP, C, BLK), BF),
            pltpu.VMEM((GX * CAP, C, BLK), BF),
            pltpu.VMEM((GX, 8, 128), F32),
            pltpu.VMEM((GX, 8, 128), F32),
            pltpu.VMEM((GY, 8, 128), F32),
            pltpu.VMEM((GX, 8, 128), F32),
            dma((GX,)), dma((GX,)), dma((8,)), dma((8,)), dma((8,)), dma((8,)),
            dma((GX,)), dma((GX,)), dma((GX,)), dma((GX,)), dma((GX,)), dma((GX,)),
            dma((GY,)), dma((GY,)), dma((GX,)), dma((GX,)),
        ],
        compiler_params=pltpu.CompilerParams(
            collective_id=0, has_side_effects=True, vmem_limit_bytes=40 * 1024 * 1024
        ),
        cost_estimate=pl.CostEstimate(
            flops=8_000_000_000, bytes_accessed=2_000_000, transcendentals=1_000_000
        ),
    )(
        inv, slot, point_counts, point_feats, point_offsets, base_cells, cotangent,
        lift_weight, conv_weight, read_weight.reshape(1, C),
    )


def solution(mesh):
    in_specs = (
        P(("gx", "gy"), None, None),
        P(("gx", "gy"), None, None),
        P(("gx", "gy"), None),
        P(("gx", "gy"), None),
        P(("gx", "gy")),
        P(),
        P(),
        P(),
        P(("gx", "gy"), None),
    )
    out_specs = (P(("gx", "gy"), None), P(("gx", "gy"), None, None), P())
    return jax.shard_map(local, mesh=mesh, in_specs=in_specs, out_specs=out_specs, check_vma=False)
```

time: 515 us -> 72.2 us (0.14)
  waiting for transfers between devices: 170 us -> 0 us
  matrix products: 120 us -> 0 us
  other arithmetic: 87.2 us -> 0 us
  Pallas kernels: 0 us -> 64.4 us
  starting transfers between devices: 62.3 us -> 0 us
  local copies, waits for them, and re-layouts: 54.2 us -> 5.99 us
  between operations: 15.5 us -> 1.39 us
    psum x1 -> x0, waiting for transfers between devices: 150 us -> none  [local(): grad_conv = lax.psum(kernel_part, ('gx', 'gy')) / slabs]
    dot_general x124 -> x0, matrix products: 120 us -> none  [the longest x32 47.6 us: add_group(): total = total + jnp.dot(high, right, preferred_element_type=jnp.float32)]
    pallas_call x0 -> x2, Pallas kernels: none -> 64.4 us  [the longest x1 62.3 us: local(): pl.pallas_call(kernel, out_shape=(jax.ShapeDtypeStruct((NB, BLK), F32), j...]
    all_to_all x6 -> x0, starting transfers between devices: 42.3 us -> none  [the longest x1 9.61 us: local(): lax.all_to_all(sampled, 'gx', split_axis=0, concat_axis=0, tiled=True)]
    mul x17 -> x0, other arithmetic: 29.6 us -> none  [the longest x16 29.6 us: add_group(): based * factor[None, None]]
    reduce_sum x5 -> x0, other arithmetic: 25.2 us -> none  [the longest x4 24.3 us: select_rows(): jnp.sum(jnp.where(shaped, rows[None], jnp.zeros((), rows.dtype)), axis=1)]
    mul x32 -> x0, local copies, waits for them, and re-layouts: 22.2 us -> none  [the longest x16 11.2 us: read_group(): along = picked_low * near_f[None, None] + picked_up * far_f[None, None]]
    ppermute x8 -> x0, starting transfers between devices: 19.9 us -> none  [the longest x4 13 us: padded_2(): lax.ppermute(tail, axis, [(i, (i + 1) % count) for i in range(ends)])]
  transfers between devices with their start and end apart: 15 -> 0, of which waited for: 4 -> 0; matrix products, arithmetic and copies ran while one was open for 46% -> 0% of each run, Pallas kernels for 0% -> 0%
where the time goes in v1:
time: 72.2 us; the launch traced here: 71.8 us
  Pallas kernels  64.4 us (89%)
  local copies, waits for them, and re-layouts  5.99 us (8%)
  between operations  1.39 us (2%)
    pallas_call x1, Pallas kernels, local(): pl.pallas_call(kernel, out_shape=(jax.ShapeDtypeStruct((NB, BLK), F32), j...  62.3 us
    unnamed x23, local copies, waits for them, and re-layouts  5.99 us
    pallas_call x1, Pallas kernels, slot_tables(): pl.pallas_call(slots_kernel, out_shape=(jax.ShapeDtypeStruct((GX * CAP,),...  2.13 us

profile of v1, /device:TPU:1, one launch (start us, length us, event | category | flops | bytes accessed | tf_op | source)
XLA Modules:
  0.0 71.8 jit_solution(17174184077079522750)
XLA Ops:
  0.6 0.0 copy-start.8
  1.3 1.3 %copy.12.owners = s32[32,1]{1,0:T(8,128)} copy(s32[32,1]{0,1:T(1,128)} %param.12) | data formatting | bytes 256 | tf_op args[3]
  2.6 2.1 %shard_map.112 = (s32[64]{0:T(128)}, s32[32]{0:T(128)}) custom-call(s32[32,1]{1,0:T(8,128)} %copy.12.owners), custom_call_target="tpu_custom_call" | custom-call | tf_op jit(solution)/shard_map/pallas_call | solution.py:50
  4.8 0.0 copy-done.8
  4.8 0.0 copy-start.2
  4.8 0.0 copy-start.3
  4.8 0.0 copy-start.4
  4.8 0.0 copy-start.5
  4.8 0.0 copy-start.6
  4.8 0.0 copy-start.7
  4.9 0.6 copy-done.2
  5.5 0.0 copy-done.3
  5.5 0.0 copy-done.4
  5.5 0.0 copy-done.5
  5.5 0.0 copy-done.6
  5.5 0.0 copy-done.7
  5.5 0.0 copy-start
  5.5 0.9 %copy-done = bf16[32,32,128]{2,1,0:T(8,128)(2,1)S(1)} copy-done((bf16[32,32,128]{2,1,0:T(8,128)(2,1)S(1)}, bf16[32,32,128]{2,1,0:T(8,128)(2,1)}, u32[]{:S(2)}) %copy-start) | copy-done | bytes 262168
  6.5 0.0 copy-start.1
  6.5 0.9 %copy-done.1 = bf16[27,32,32]{2,1,0:T(8,128)(2,1)S(1)} copy-done((bf16[27,32,32]{2,1,0:T(8,128)(2,1)S(1)}, bf16[27,32,32]{2,1,0:T(8,128)(2,1)}, u32[]{:S(2)}) %copy-start.1) | copy-done | bytes 55320
  7.4 62.3 %shard_map.113 = (f32[32,128]{1,0:T(8,128)S(1)}, bf16[32,32,128]{2,1,0:T(8,128)(2,1)S(1)}, f32[27,32,32]{2,1,0:T(8,128)S(1)}) custom-call(s32[64]{0:T(128)S(1)} %copy-done.6, s32[32]{0:T(128)S(1)} %copy-done.7, s32[1]{0:T(128)S(6)} %copy.17.count, bf16[32,32,128]{2,1,0:T(8,128)(2,1)S(1)} %copy-done, bf16[32,3,128]{2,1,0:T(4,128)(2,1)S(1)} %copy.13.offsets, ...), custom_call_target="tpu_custom_call" | custom-call | flops 8000000000 | bytes 2000000 | tf_op jit(solution)/shard_map/pallas_call | solution.py:486
  69.7 0.6 copy.18
  70.3 0.7 copy.19
  71.0 0.8 %copy.20 = f32[27,32,32]{2,1,0:T(8,128)} copy(f32[27,32,32]{2,1,0:T(8,128)S(1)} %get-tuple-element.12) | data formatting | bytes 221184
  (1 shorter events, 0.0 us)
Async XLA Ops:
  0.6 4.1 %copy-start.8 = (bf16[32,3,128]{2,0,1:T(8,128)(2,1)S(1)}, bf16[32,3,128]{2,0,1:T(8,128)(2,1)}, u32[]{:S(2)}) copy-start(bf16[32,3,128]{2,0,1:T(8,128)(2,1)} %param.10) | copy-start | bytes 73732
  4.8 0.7 %copy-start.2 = (s32[32,128]{1,0:T(8,128)S(1)}, s32[32,128]{1,0:T(8,128)}, u32[]{:S(2)}) copy-start(s32[32,128]{1,0:T(8,128)} %base.1) | copy-start | bytes 49156
  4.8 0.7 %copy-start.3 = (f32[32,128]{1,0:T(8,128)S(1)}, f32[32,128]{1,0:T(8,128)}, u32[]{:S(2)}) copy-start(f32[32,128]{1,0:T(8,128)} %cot.1) | copy-start | bytes 49156
  4.8 0.7 copy-start.4
  4.8 0.7 copy-start.5
  4.8 0.7 copy-start.6
  4.8 0.7 copy-start.7
  5.5 1.0 %copy-start = (bf16[32,32,128]{2,1,0:T(8,128)(2,1)S(1)}, bf16[32,32,128]{2,1,0:T(8,128)(2,1)}, u32[]{:S(2)}) copy-start(bf16[32,32,128]{2,1,0:T(8,128)(2,1)} %feats.1) | copy-start | bytes 786436
  6.5 0.9 %copy-start.1 = (bf16[27,32,32]{2,1,0:T(8,128)(2,1)S(1)}, bf16[27,32,32]{2,1,0:T(8,128)(2,1)}, u32[]{:S(2)}) copy-start(bf16[27,32,32]{2,1,0:T(8,128)(2,1)} %conv.1) | copy-start | bytes 165892

commit v2 on v1

--- a/solution.py
+++ b/solution.py
@@ -17,6 +17,9 @@
 GY = 4
 CAP = 2
 PTS = CAP * BLK
+GROUP = 4
+GROUPS = GX // GROUP
+WIDE = GROUP * PTS
 COLS = CX * CY
 TAPS = 27
 MESH = pl.DeviceIdType.MESH
@@ -28,37 +31,6 @@
     return lax.dot_general(a, b, (((ca,), (cb,)), ((), ())), preferred_element_type=F32)
 
 
-def slots_kernel(owners, inv, slot, cnt):
-    @pl.loop(0, GX)
-    def _(o):
-        cnt[o] = 0
-        inv[CAP * o] = -1
-        inv[CAP * o + 1] = -1
-
-    @pl.loop(0, NB)
-    def _(j):
-        o = owners[j, 0]
-        r = cnt[o]
-        cnt[o] = r + 1
-        s = CAP * o + r
-        inv[s] = j
-        slot[j] = s
-
-
-def slot_tables(owners):
-    smem = pl.BlockSpec(memory_space=pltpu.SMEM)
-    return pl.pallas_call(
-        slots_kernel,
-        out_shape=(
-            jax.ShapeDtypeStruct((GX * CAP,), jnp.int32),
-            jax.ShapeDtypeStruct((NB,), jnp.int32),
-        ),
-        in_specs=[smem],
-        out_specs=(smem, smem),
-        scratch_shapes=[pltpu.SMEM((GX,), jnp.int32)],
-    )(owners)
-
-
 def shifted(values, step):
     lanes = lax.broadcasted_iota(jnp.int32, values.shape, 1)
     if step == 1:
@@ -73,9 +45,9 @@
 
 
 def kernel(
-    inv, slot, count, feats, offsets, base, cot, lift, conv, read,
+    feats_hbm, offsets_hbm, base_hbm, owners_hbm, count_hbm, lift_hbm, conv_hbm, read_hbm, cot_hbm,
     pred_out, feats_out, conv_out,
-    bmat, cmat, ghi, glo, send, recv, acc, zs, planes, latp, gp, gs, wf, wb,
+    feats, offsets, base, owners, count, lift, conv, read, cot, table, slots, aux, in_sem, send, recv, acc, zs, planes, latp, gp, gs, wf, wb,
     gout, field, gl, predmsg, predr, gfs, gfr, redsrc, red1, red2, red3,
     s_send, s_recv, h_send, h_recv, i_send, i_recv, p_send, p_recv,
     f_send, f_recv, a_send, a_recv, b_send, b_recv, c_send, c_recv,
@@ -85,6 +57,18 @@
     right, left = lax.rem(mx + 1, GX), lax.rem(mx + GX - 1, GX)
     up, down = lax.rem(my + 1, GY), lax.rem(my + GY - 1, GY)
 
+    pairs = {
+        "owners": (owners_hbm, owners), "offsets": (offsets_hbm, offsets), "base": (base_hbm, base),
+        "count": (count_hbm, count), "cot": (cot_hbm, cot), "feats": (feats_hbm, feats),
+        "lift": (lift_hbm, lift), "conv": (conv_hbm, conv), "read": (read_hbm, read),
+    }
+    fetched = {
+        name: pltpu.make_async_copy(src, dst, in_sem.at[n])
+        for n, (name, (src, dst)) in enumerate(pairs.items())
+    }
+    for copy in fetched.values():
+        copy.start()
+
     barrier = pltpu.get_barrier_semaphore()
 
     @pl.loop(1, GX)
@@ -97,46 +81,46 @@
         for py in (down, up):
             pl.semaphore_signal(barrier, inc=1, device_id=(px, py), device_id_type=MESH)
 
+    fetched["owners"].wait()
+    named = owners[...]
+    rows32 = lax.broadcasted_iota(jnp.int32, (NB, NB), 0)
+    lanes32 = lax.broadcasted_iota(jnp.int32, (NB, NB), 1)
+    named_col = jnp.sum(jnp.where(rows32 == lanes32, named, 0), axis=1, keepdims=True)
+    earlier = (named_col == named) & (rows32 < lanes32)
+    slot_row = CAP * named + jnp.sum(jnp.where(earlier, 1, 0), axis=0, keepdims=True)
+    slot_col = jnp.sum(jnp.where(rows32 == lanes32, slot_row, 0), axis=1, keepdims=True)
+    rows = lax.broadcasted_iota(jnp.int32, (NB, BLK), 0)
+    lanes = lax.broadcasted_iota(jnp.int32, (NB, BLK), 1)
+    table[0:1, :] = jnp.sum(jnp.where(slot_col == lanes, rows + 1, 0), axis=0, keepdims=True) - 1
+    table[1:2, :] = jnp.sum(jnp.where(rows == lanes, slot_col, 0), axis=0, keepdims=True)
+    table[2:8, :] = jnp.zeros((6, BLK), jnp.int32)
+    to_slots = pltpu.make_async_copy(table, slots, in_sem.at[9])
+    to_slots.start()
+
+    for name in ("offsets", "base", "count", "cot"):
+        fetched[name].wait()
     cells = base[...].astype(F32)
-    rows_b = jnp.floor((cells + 0.5) * (1.0 / (NZ - 1)))
-    bmat[...] = rows_b
-    cmat[...] = cells - rows_b * (NZ - 1.0)
-    live_count = count[0]
-    position = lax.broadcasted_iota(jnp.int32, (NB, BLK), 0) * BLK + lax.broadcasted_iota(
-        jnp.int32, (NB, BLK), 1
-    )
-    grad = jnp.where(position < live_count, cot[...], 0.0)
+    cell_y = jnp.floor((cells + 0.5) * (1.0 / (NZ - 1)))
+    alive = jnp.where(rows * BLK + lanes < count[...], 1.0, 0.0)
+    grad = cot[...] * alive
     high = grad.astype(BF).astype(F32)
-    ghi[...] = high
-    glo[...] = grad - high
-    lane32 = lax.broadcasted_iota(jnp.int32, (C, BLK), 1)
-    sub8 = lax.broadcasted_iota(jnp.int32, (8, BLK), 0)
+    tile_rows = [offsets[n].astype(F32) for n in range(3)]
+    tile_rows += [cell_y, cells - cell_y * (NZ - 1.0), high, grad - high, alive]
+    for n, value in enumerate(tile_rows):
+        aux[:, n, :] = value
+    fetched["feats"].wait()
+    to_slots.wait()
 
     def place(o):
         tails = []
         for r in range(CAP):
-            j = inv[CAP * o + r]
+            j = slots[0, CAP * o + r]
             jj = jnp.maximum(j, 0)
-            live = jnp.where(j >= 0, live_count - jj * BLK, 0)
-            block = jnp.where(lane32 < live, feats[jj].astype(F32), 0.0)
-            send[o, r * C : (r + 1) * C, :] = block.astype(BF)
-            off = offsets[jj].astype(F32)
             here = jnp.where(j >= 0, 1.0, 0.0)
-            tail = jnp.where(sub8 == 0, off[0:1], 0.0)
-            tail = jnp.where(sub8 == 1, off[1:2], tail)
-            tail = jnp.where(sub8 == 2, off[2:3], tail)
-            tail = jnp.where(sub8 == 3, bmat[pl.ds(jj, 1), :], tail)
-            tail = jnp.where(sub8 == 4, cmat[pl.ds(jj, 1), :], tail)
-            tail = jnp.where(sub8 == 5, ghi[pl.ds(jj, 1), :] * here, tail)
-            tail = jnp.where(sub8 == 6, glo[pl.ds(jj, 1), :] * here, tail)
+            tail = aux[jj] * here
+            send[o, r * C : (r + 1) * C, :] = (feats[jj].astype(F32) * tail[7:8]).astype(BF)
             tails.append(tail)
         send[o, CAP * C : CAP * C + 16, :] = jnp.concatenate(tails, axis=0).astype(BF)
-
-    @pl.loop(0, GX)
-    def _(o):
-        place(o)
-
-    pl.semaphore_wait(barrier, GX - 1 + GY - 1 + 4)
 
     def points_copy(k):
         to = lax.rem(mx + k, GX)
@@ -146,10 +130,18 @@
             device_id=(to, my), device_id_type=MESH,
         )
 
-    @pl.loop(1, GX)
-    def _(k):
+    pl.semaphore_wait(barrier, GX - 1 + GY - 1 + 4)
+
+    @pl.loop(1, GX)
+    def _(k):
+        place(lax.rem(mx + k, GX))
         points_copy(k).start()
 
+    place(mx)
+    recv[mx] = send[mx]
+
+    for name in ("lift", "conv", "read"):
+        fetched[name].wait()
     def place_tap(xp):
         lanes = lax.broadcasted_iota(jnp.int32, (C, 128), 1)
         rows = lax.broadcasted_iota(jnp.int32, (C, 128), 0)
@@ -180,37 +172,47 @@
     read_col = dot((eye * read[...].astype(F32)).astype(BF), jnp.ones((C, NZ), BF))
     lift_w = lift[...]
 
-    sub_z = lax.broadcasted_iota(jnp.int32, (NZ, PTS), 0).astype(F32)
-    sub_y = lax.broadcasted_iota(jnp.int32, (CY, PTS), 0).astype(F32)
-
-    def spread(msg, k):
-        block = jnp.concatenate([msg[0:C], msg[C : 2 * C]], axis=1)
-        tail = msg[2 * C : 2 * C + 16].astype(F32)
-        tail = jnp.concatenate([tail[0:8], tail[8:16]], axis=1)
+    sub_z = lax.broadcasted_iota(jnp.int32, (NZ, WIDE), 0).astype(F32)
+    sub_y = lax.broadcasted_iota(jnp.int32, (CY, WIDE), 0).astype(F32)
+    acc[...] = jnp.zeros(acc.shape, F32)
+
+    @pl.loop(0, GROUPS)
+    def _(g):
+        blocks, tails = [], []
+        for n in range(GROUP):
+            k = GROUP * g + n
+            if n == 0:
+
+                @pl.when(g > 0)
+                def _():
+                    points_copy(GROUP * g).wait_recv()
+
+            else:
+                points_copy(k).wait_recv()
+        for n in range(GROUP):
+            msg = recv[lax.rem(mx - (GROUP * g + n) + GX, GX)]
+            blocks += [msg[0:C], msg[C : 2 * C]]
+            tail = msg[2 * C : 2 * C + 16].astype(F32)
+            tails += [tail[0:8], tail[8:16]]
+        block = jnp.concatenate(blocks, axis=1)
+        tail = jnp.concatenate(tails, axis=1)
         near = jnp.exp(-2.0 * tail * tail)
         far = jnp.exp(-2.0 * (tail - 1.0) * (tail - 1.0))
         at_y, at_z = tail[3:4], tail[4:5]
         slope = tail[5:6] + tail[6:7]
         wy = jnp.where(sub_y == at_y, near[1:2], jnp.where(sub_y == at_y + 1.0, far[1:2], 0.0))
         plane = (near[0:1] * wy, far[0:1] * wy)
-        planes[k, 0:CY, :] = plane[0]
-        planes[k, CY : 2 * CY, :] = plane[1]
+        planes[g, 0:CY, :] = plane[0]
+        planes[g, CY : 2 * CY, :] = plane[1]
         z = jnp.where(sub_z == at_z, near[2:3], jnp.where(sub_z == at_z + 1.0, far[2:3], 0.0))
         z = z.astype(BF)
-        zs[k] = z
+        zs[g] = z
         lifted = dot(lift_w, block, 0, 0).astype(BF).astype(F32)
         rows = [
             (lifted * plane[x][y : y + 1]).astype(BF) for y in range(CY) for x in range(CX)
         ]
         rows.append(jnp.concatenate([plane[0] * slope, plane[1] * slope], axis=0).astype(BF))
-        return dot(jnp.concatenate(rows, axis=0), z, 1, 1)
-
-    acc[...] = spread(send[mx], 0)
-
-    @pl.loop(1, GX)
-    def _(k):
-        points_copy(k).wait_recv()
-        acc[...] += spread(recv[lax.rem(mx - k + GX, GX)], k)
+        acc[...] += dot(jnp.concatenate(rows, axis=0), z, 1, 1)
 
     def halo_copies(buf, sends, recvs):
         ends = (
@@ -332,11 +334,6 @@
     scalar_lo = (scalar - scalar_hi.astype(F32)).astype(BF)
     scalars = jnp.concatenate([scalar_hi, scalar_lo], axis=0)
 
-    def read_points(k):
-        got = dot(scalars, zs[k])
-        total = jnp.sum((got[0:COLS] + got[COLS:]) * planes[k], axis=0, keepdims=True)
-        return total[:, 0:BLK], total[:, BLK:]
-
     def pred_copy(k):
         to = lax.rem(mx - k + GX, GX)
         return pltpu.make_async_remote_copy(
@@ -345,17 +342,26 @@
             device_id=(to, my), device_id_type=MESH,
         )
 
-    first, second = read_points(0)
-    predr[mx, 0:1, :] = first
-    predr[mx, 1:2, :] = second
-
-    @pl.loop(1, GX)
-    def _(k):
-        one, two = read_points(k)
-        predmsg[k, 0:1, :] = one
-        predmsg[k, 1:2, :] = two
-        predmsg[k, 2:8, :] = jnp.zeros((6, BLK), F32)
-        pred_copy(k).start()
+    @pl.loop(0, GROUPS)
+    def _(g):
+        got = dot(scalars, zs[g])
+        total = jnp.sum((got[0:COLS] + got[COLS:]) * planes[g], axis=0, keepdims=True)
+        for n in range(GROUP):
+            k = GROUP * g + n
+            for r in range(CAP):
+                lane = n * PTS + r * BLK
+                predmsg[k, r : r + 1, :] = total[:, lane : lane + BLK]
+            predmsg[k, CAP:8, :] = jnp.zeros((8 - CAP, BLK), F32)
+            if n == 0:
+
+                @pl.when(g > 0)
+                def _():
+                    pred_copy(GROUP * g).start()
+
+            else:
+                pred_copy(k).start()
+
+    predr[mx] = predmsg[0]
 
     for copy in halos2:
         copy.wait_recv()
@@ -386,16 +392,6 @@
     for k in range(1, GY):
         rows_copy(k).start()
 
-    def gather(k):
-        got = dot(gl[...], zs[k])
-        total = jnp.zeros((C, PTS), F32)
-        for y in range(CY):
-            for x in range(CX):
-                n = (y * CX + x) * C
-                total = total + got[n : n + C] * planes[k, x * CY + y : x * CY + y + 1, :]
-        back = dot(lift_w, total.astype(BF)).astype(BF)
-        return back[:, 0:BLK], back[:, BLK:]
-
     def feats_copy(k):
         to = lax.rem(mx - k + GX, GX)
         return pltpu.make_async_remote_copy(
@@ -404,15 +400,31 @@
             device_id=(to, my), device_id_type=MESH,
         )
 
-    def send_back(k):
-        one, two = gather(k)
-        gfs[k, 0] = one
-        gfs[k, 1] = two
-        feats_copy(k).start()
-
-    @pl.loop(1, 12)
-    def _(k):
-        send_back(k)
+    def send_back(g):
+        got = dot(gl[...], zs[g])
+        total = jnp.zeros((C, WIDE), F32)
+        for y in range(CY):
+            for x in range(CX):
+                n = (y * CX + x) * C
+                total = total + got[n : n + C] * planes[g, x * CY + y : x * CY + y + 1, :]
+        back = dot(lift_w, total.astype(BF)).astype(BF)
+        for n in range(GROUP):
+            k = GROUP * g + n
+            for r in range(CAP):
+                lane = n * PTS + r * BLK
+                gfs[k, r] = back[:, lane : lane + BLK]
+            if n == 0:
+
+                @pl.when(g > 0)
+                def _():
+                    feats_copy(GROUP * g).start()
+
+            else:
+                feats_copy(k).start()
+
+    @pl.loop(1, 4)
+    def _(g):
+        send_back(g)
 
     for k in range(1, GY):
         rows_copy(k).wait_recv()
@@ -432,13 +444,11 @@
     def _(k):
         total_copy(k).start()
 
-    @pl.loop(12, GX)
-    def _(k):
-        send_back(k)
-
-    first_gf, second_gf = gather(0)
-    gfr[CAP * mx] = first_gf
-    gfr[CAP * mx + 1] = second_gf
+    @pl.loop(4, GROUPS + 1)
+    def _(g):
+        send_back(lax.rem(g, GROUPS))
+
+    gfr[pl.ds(CAP * mx, CAP)] = gfs[0]
 
     @pl.loop(1, GX)
     def _(k):
@@ -455,16 +465,14 @@
     def _(k):
         feats_copy(k).wait_recv()
 
-    lane1 = lax.broadcasted_iota(jnp.int32, (1, BLK), 1)
-
     @pl.loop(0, NB)
     def _(j):
-        s = slot[j]
-        live = live_count - j * BLK
-        feats_out[j] = jnp.where(lane32 < live, gfr[s].astype(F32), 0.0).astype(BF)
+        s = slots[1, j]
+        keep = aux[j, 7:8, :]
+        feats_out[j] = (gfr[s].astype(F32) * keep).astype(BF)
         both = predr[s // CAP]
         value = jnp.where(lax.rem(s, CAP) == 0, both[0:1], both[1:2])
-        pred_out[pl.ds(j, 1), :] = jnp.where(lane1 < live, value, 0.0)
+        pred_out[pl.ds(j, 1), :] = value * keep
 
     @pl.loop(1, GX)
     def _(k):
@@ -479,8 +487,7 @@
     point_feats, point_offsets, base_cells, block_owners, point_counts,
     lift_weight, conv_weight, read_weight, cotangent,
 ):
-    inv, slot = slot_tables(block_owners)
-    smem = pl.BlockSpec(memory_space=pltpu.SMEM)
+    hbm = pl.BlockSpec(memory_space=pltpu.HBM)
     vmem = pl.BlockSpec(memory_space=pltpu.VMEM)
     dma = pltpu.SemaphoreType.DMA
     return pl.pallas_call(
@@ -490,18 +497,27 @@
             jax.ShapeDtypeStruct((NB, C, BLK), BF),
             jax.ShapeDtypeStruct((TAPS, C, C), F32),
         ),
-        in_specs=[smem, smem, smem] + [vmem] * 7,
+        in_specs=[hbm] * 9,
         out_specs=(vmem, vmem, vmem),
         scratch_shapes=[
+            pltpu.VMEM((NB, C, BLK), BF),
+            pltpu.VMEM((3, NB, BLK), BF),
+            pltpu.VMEM((NB, BLK), jnp.int32),
+            pltpu.VMEM((1, NB), jnp.int32),
+            pltpu.VMEM((1, 1), jnp.int32),
+            pltpu.VMEM((C, C), BF),
+            pltpu.VMEM((TAPS, C, C), BF),
+            pltpu.VMEM((1, C), BF),
             pltpu.VMEM((NB, BLK), F32),
-            pltpu.VMEM((NB, BLK), F32),
-            pltpu.VMEM((NB, BLK), F32),
-            pltpu.VMEM((NB, BLK), F32),
+            pltpu.VMEM((8, BLK), jnp.int32),
+            pltpu.SMEM((8, BLK), jnp.int32),
+            pltpu.VMEM((NB, 8, BLK), F32),
+            dma((10,)),
             pltpu.VMEM((GX, CAP * C + 16, BLK), BF),
             pltpu.VMEM((GX, CAP * C + 16, BLK), BF),
             pltpu.VMEM((COLS * C + COLS, NZ), F32),
-            pltpu.VMEM((GX, NZ, PTS), BF),
-            pltpu.VMEM((GX, COLS, PTS), F32),
+            pltpu.VMEM((GROUPS, NZ, WIDE), BF),
+            pltpu.VMEM((GROUPS, COLS, WIDE), F32),
             pltpu.VMEM((10, 4, C, NZ), BF),
             pltpu.VMEM((10, 4, C, NZ), BF),
             pltpu.VMEM((4, 3 * 128, NZ), BF),
@@ -523,14 +539,15 @@
             dma((GY,)), dma((GY,)), dma((GX,)), dma((GX,)),
         ],
         compiler_params=pltpu.CompilerParams(
-            collective_id=0, has_side_effects=True, vmem_limit_bytes=40 * 1024 * 1024
+            collective_id=0, has_side_effects=True, vmem_limit_bytes=63 * 1024 * 1024
         ),
         cost_estimate=pl.CostEstimate(
             flops=8_000_000_000, bytes_accessed=2_000_000, transcendentals=1_000_000
         ),
     )(
-        inv, slot, point_counts, point_feats, point_offsets, base_cells, cotangent,
-        lift_weight, conv_weight, read_weight.reshape(1, C),
+        point_feats, jnp.transpose(point_offsets, (1, 0, 2)), base_cells,
+        block_owners.reshape(1, NB), point_counts.reshape(1, 1), lift_weight, conv_weight,
+        read_weight.reshape(1, C), cotangent,
     )
 
 

time: 72.2 us -> 60.8 us (0.84)
  Pallas kernels: 64.4 us -> 55.5 us
  local copies, waits for them, and re-layouts: 5.99 us -> 3.81 us
    pallas_call x1, Pallas kernels: 62.3 us -> 55.5 us  [local(): pl.pallas_call(kernel, out_shape=(jax.ShapeDtypeStruct((NB, BLK), F32), j...]
    unnamed x23 -> x5, local copies, waits for them, and re-layouts: 5.99 us -> 3.81 us
    pallas_call x1 -> x0, Pallas kernels: 2.13 us -> none  [slot_tables(): pl.pallas_call(slots_kernel, out_shape=(jax.ShapeDtypeStruct((GX * CAP,),...]
where the time goes in v2:
time: 60.8 us; the launch traced here: 60.6 us
  Pallas kernels  55.5 us (91%)
  local copies, waits for them, and re-layouts  3.81 us (6%)
  between operations  1.3 us (2%)
    pallas_call x1, Pallas kernels, local(): pl.pallas_call(kernel, out_shape=(jax.ShapeDtypeStruct((NB, BLK), F32), j...  55.5 us
    unnamed x5, local copies, waits for them, and re-layouts  3.81 us

profile of v2, /device:TPU:1, one launch (start us, length us, event | category | flops | bytes accessed | tf_op | source)
XLA Modules:
  0.0 60.6 jit_solution(17167463869809522088)
XLA Ops:
  1.3 55.5 %shard_map.112 = (f32[32,128]{1,0:T(8,128)}, bf16[32,32,128]{2,1,0:T(8,128)(2,1)}, f32[27,32,32]{2,1,0:T(8,128)}) custom-call(bf16[32,32,128]{2,1,0:T(8,128)(2,1)} %feats_hbm.1, bf16[3,32,128]{2,1,0:T(8,128)(2,1)} %bitcast.5, s32[32,128]{1,0:T(8,128)} %base_hbm.1, s32[1,32]{1,0:T(1,128)} %bitcast.6, s32[1,1]{1,0:T(1,128)} %bitcast.4.count_hbm, ...), custom_call_target="tpu_custom_call" | custom-call | flops 8000000000 | bytes 2000000 | tf_op jit(solution)/shard_map/pallas_call | solution.py:493
  56.8 0.0 copy-start
  56.8 1.4 %copy.16 = f32[32,128]{1,0:T(8,128)} copy(f32[32,128]{1,0:T(8,128)} %get-tuple-element.6) | data formatting | bytes 32768
  58.2 1.7 %copy.17 = bf16[32,32,128]{2,1,0:T(8,128)(2,1)} copy(bf16[32,32,128]{2,1,0:T(8,128)(2,1)} %get-tuple-element.7) | data formatting | bytes 524288
  59.9 0.0 copy-done
  59.9 0.8 %copy.18 = f32[27,32,32]{2,1,0:T(8,128)} copy(f32[27,32,32]{2,1,0:T(8,128)S(1)} %copy-done) | data formatting | bytes 221184
Async XLA Ops:
  56.8 3.1 %copy-start = (f32[27,32,32]{2,1,0:T(8,128)S(1)}, f32[27,32,32]{2,1,0:T(8,128)}, u32[]{:S(2)}) copy-start(f32[27,32,32]{2,1,0:T(8,128)} %get-tuple-element.8) | copy-start | bytes 331780

commit v3 on v2

--- a/solution.py
+++ b/solution.py
@@ -46,9 +46,9 @@
 
 def kernel(
     feats_hbm, offsets_hbm, base_hbm, owners_hbm, count_hbm, lift_hbm, conv_hbm, read_hbm, cot_hbm,
-    pred_out, feats_out, conv_out,
-    feats, offsets, base, owners, count, lift, conv, read, cot, table, slots, aux, in_sem, send, recv, acc, zs, planes, latp, gp, gs, wf, wb,
-    gout, field, gl, predmsg, predr, gfs, gfr, redsrc, red1, red2, red3,
+    gfr, predr, red3, alive_out, table,
+    feats, offsets, base, owners, count, lift, conv, read, cot, slots, aux, in_sem, send, recv, acc, zs, planes, latp, gp, gs, wf, wb,
+    gout, field, gl, predmsg, gfs, redsrc, red1, red2,
     s_send, s_recv, h_send, h_recv, i_send, i_recv, p_send, p_recv,
     f_send, f_recv, a_send, a_recv, b_send, b_recv, c_send, c_recv,
 ):
@@ -102,6 +102,7 @@
     cells = base[...].astype(F32)
     cell_y = jnp.floor((cells + 0.5) * (1.0 / (NZ - 1)))
     alive = jnp.where(rows * BLK + lanes < count[...], 1.0, 0.0)
+    alive_out[...] = alive
     grad = cot[...] * alive
     high = grad.astype(BF).astype(F32)
     tile_rows = [offsets[n].astype(F32) for n in range(3)]
@@ -142,29 +143,6 @@
 
     for name in ("lift", "conv", "read"):
         fetched[name].wait()
-    def place_tap(xp):
-        lanes = lax.broadcasted_iota(jnp.int32, (C, 128), 1)
-        rows = lax.broadcasted_iota(jnp.int32, (C, 128), 0)
-        return jnp.where(lanes == rows + C * xp, 1.0, 0.0).astype(BF)
-
-    spots = [place_tap(xp) for xp in range(4)]
-    wf[...] = jnp.zeros(wf.shape, BF)
-    wb[...] = jnp.zeros(wb.shape, BF)
-    for dz in range(3):
-        for dy in range(3):
-            for xo in range(2):
-                tile_f = sum(
-                    dot(conv[9 * dx + 3 * dy + dz], spots[dx + xo], 0, 0) for dx in range(3)
-                ).astype(BF)
-                tile_b = sum(
-                    dot(conv[9 * (2 - dx) + 3 * (2 - dy) + (2 - dz)], spots[dx + xo])
-                    for dx in range(3)
-                ).astype(BF)
-                for yo in range(2):
-                    row = ((dz * 2 + yo) * 2 + xo) * C
-                    lane = (yo + dy) * 128
-                    wf[row : row + C, lane : lane + 128] = tile_f
-                    wb[row : row + C, lane : lane + 128] = tile_b
     eye = jnp.where(
         lax.broadcasted_iota(jnp.int32, (C, C), 0) == lax.broadcasted_iota(jnp.int32, (C, C), 1),
         1.0, 0.0,
@@ -257,6 +235,30 @@
     halos = halo_copies(latp, h_send, h_recv)
     for copy in halos:
         copy.start()
+
+    def place_tap(xp):
+        lanes = lax.broadcasted_iota(jnp.int32, (C, 128), 1)
+        rows = lax.broadcasted_iota(jnp.int32, (C, 128), 0)
+        return jnp.where(lanes == rows + C * xp, 1.0, 0.0).astype(BF)
+
+    spots = [place_tap(xp) for xp in range(4)]
+    wf[...] = jnp.zeros(wf.shape, BF)
+    wb[...] = jnp.zeros(wb.shape, BF)
+    for dz in range(3):
+        for dy in range(3):
+            for xo in range(2):
+                tile_f = sum(
+                    dot(conv[9 * dx + 3 * dy + dz], spots[dx + xo], 0, 0) for dx in range(3)
+                ).astype(BF)
+                tile_b = sum(
+                    dot(conv[9 * (2 - dx) + 3 * (2 - dy) + (2 - dz)], spots[dx + xo])
+                    for dx in range(3)
+                ).astype(BF)
+                for yo in range(2):
+                    row = ((dz * 2 + yo) * 2 + xo) * C
+                    lane = (yo + dy) * 128
+                    wf[row : row + C, lane : lane + 128] = tile_f
+                    wb[row : row + C, lane : lane + 128] = tile_b
     for copy in halos:
         copy.wait_recv()
     for copy in halos:
@@ -337,7 +339,7 @@
     def pred_copy(k):
         to = lax.rem(mx - k + GX, GX)
         return pltpu.make_async_remote_copy(
-            src_ref=predmsg.at[k], dst_ref=predr.at[mx],
+            src_ref=predmsg.at[k, 0:CAP], dst_ref=predr.at[mx, 0:CAP],
             send_sem=p_send.at[k], recv_sem=p_recv.at[k],
             device_id=(to, my), device_id_type=MESH,
         )
@@ -351,7 +353,6 @@
             for r in range(CAP):
                 lane = n * PTS + r * BLK
                 predmsg[k, r : r + 1, :] = total[:, lane : lane + BLK]
-            predmsg[k, CAP:8, :] = jnp.zeros((8 - CAP, BLK), F32)
             if n == 0:
 
                 @pl.when(g > 0)
@@ -361,7 +362,7 @@
             else:
                 pred_copy(k).start()
 
-    predr[mx] = predmsg[0]
+    predr[mx, 0:CAP, :] = predmsg[0, 0:CAP, :]
 
     for copy in halos2:
         copy.wait_recv()
@@ -374,30 +375,19 @@
             gout[128 * pair : 128 * pair + 128, :] + back
         ).astype(BF)
 
-    red1[mx] = redsrc[mx]
-
-    @pl.loop(1, GX)
-    def _(k):
-        taps_copy(k).wait_recv()
-
-    red2[my] = jnp.sum(red1[...], axis=0)
-
-    def rows_copy(k):
-        return pltpu.make_async_remote_copy(
-            src_ref=red2.at[my], dst_ref=red2.at[my],
-            send_sem=b_send.at[k], recv_sem=b_recv.at[k],
-            device_id=(mx, lax.rem(my + k, GY)), device_id_type=MESH,
-        )
-
-    for k in range(1, GY):
-        rows_copy(k).start()
-
     def feats_copy(k):
         to = lax.rem(mx - k + GX, GX)
         return pltpu.make_async_remote_copy(
             src_ref=gfs.at[k], dst_ref=gfr.at[pl.ds(CAP * mx, CAP)],
             send_sem=f_send.at[k], recv_sem=f_recv.at[k],
             device_id=(to, my), device_id_type=MESH,
+        )
+
+    def rows_copy(k):
+        return pltpu.make_async_remote_copy(
+            src_ref=red2.at[my], dst_ref=red2.at[my],
+            send_sem=b_send.at[k], recv_sem=b_recv.at[k],
+            device_id=(mx, lax.rem(my + k, GY)), device_id_type=MESH,
         )
 
     def send_back(g):
@@ -426,6 +416,20 @@
     def _(g):
         send_back(g)
 
+    red1[mx] = redsrc[mx]
+
+    @pl.loop(1, GX)
+    def _(k):
+        taps_copy(k).wait_recv()
+
+    red2[my] = jnp.sum(red1[...], axis=0)
+    for k in range(1, GY):
+        rows_copy(k).start()
+
+    @pl.loop(4, GROUPS)
+    def _(g):
+        send_back(g)
+
     for k in range(1, GY):
         rows_copy(k).wait_recv()
     for k in range(1, GY):
@@ -444,43 +448,50 @@
     def _(k):
         total_copy(k).start()
 
-    @pl.loop(4, GROUPS + 1)
-    def _(g):
-        send_back(lax.rem(g, GROUPS))
-
+    send_back(0)
     gfr[pl.ds(CAP * mx, CAP)] = gfs[0]
 
     @pl.loop(1, GX)
     def _(k):
-        pred_copy(k).wait_recv()
-        total_copy(k).wait_recv()
-
+        pred_copy(k).wait()
+        total_copy(k).wait()
+        feats_copy(k).wait()
+        points_copy(k).wait_send()
+        taps_copy(k).wait_send()
+
+
+def finish_kernel(
+    gfr, predr, red3, alive, table, pred_out, feats_out, conv_out,
+    slots, pred, feats, conv, sems,
+):
+    to_slots = pltpu.make_async_copy(table, slots, sems.at[0])
+    to_slots.start()
     for d in range(TAPS):
         packed = red3[d]
         for q in range(4):
             piece = packed if q == 0 else pltpu.roll(packed, 128 - C * q, 1)
-            conv_out[d, 8 * q : 8 * q + 8, :] = piece[:, 0:C]
-
-    @pl.loop(1, GX)
-    def _(k):
-        feats_copy(k).wait_recv()
-
-    @pl.loop(0, NB)
-    def _(j):
-        s = slots[1, j]
-        keep = aux[j, 7:8, :]
-        feats_out[j] = (gfr[s].astype(F32) * keep).astype(BF)
-        both = predr[s // CAP]
-        value = jnp.where(lax.rem(s, CAP) == 0, both[0:1], both[1:2])
-        pred_out[pl.ds(j, 1), :] = value * keep
-
-    @pl.loop(1, GX)
-    def _(k):
-        points_copy(k).wait_send()
-        taps_copy(k).wait_send()
-        pred_copy(k).wait_send()
-        feats_copy(k).wait_send()
-        total_copy(k).wait_send()
+            conv[d, 8 * q : 8 * q + 8, :] = piece[:, 0:C]
+    copies = [pltpu.make_async_copy(conv, conv_out, sems.at[1])]
+    copies[0].start()
+    to_slots.wait()
+    for part in range(4):
+
+        @pl.loop(8 * part, 8 * part + 8)
+        def _(j):
+            s = slots[1, j]
+            keep = alive[pl.ds(j, 1), :]
+            feats[j] = (gfr[s].astype(F32) * keep).astype(BF)
+            both = predr[s // CAP]
+            value = jnp.where(lax.rem(s, CAP) == 0, both[0:1], both[1:2])
+            pred[pl.ds(j, 1), :] = value * keep
+
+        span = pl.ds(8 * part, 8)
+        copies.append(pltpu.make_async_copy(feats.at[span], feats_out.at[span], sems.at[2 + part]))
+        copies[-1].start()
+    copies.append(pltpu.make_async_copy(pred, pred_out, sems.at[6]))
+    copies[-1].start()
+    for copy in copies:
+        copy.wait()
 
 
 def local(
@@ -490,15 +501,22 @@
     hbm = pl.BlockSpec(memory_space=pltpu.HBM)
     vmem = pl.BlockSpec(memory_space=pltpu.VMEM)
     dma = pltpu.SemaphoreType.DMA
-    return pl.pallas_call(
+    inputs = (
+        point_feats, jnp.transpose(point_offsets, (1, 0, 2)), base_cells,
+        block_owners.reshape(1, NB), point_counts.reshape(1, 1), lift_weight, conv_weight,
+        read_weight.reshape(1, C), cotangent,
+    )
+    parts = pl.pallas_call(
         kernel,
         out_shape=(
-            jax.ShapeDtypeStruct((NB, BLK), F32),
-            jax.ShapeDtypeStruct((NB, C, BLK), BF),
-            jax.ShapeDtypeStruct((TAPS, C, C), F32),
+            pltpu.VMEM((GX * CAP, C, BLK), BF),
+            pltpu.VMEM((GX, 8, BLK), F32),
+            pltpu.VMEM((GX, 8, 128), F32),
+            pltpu.VMEM((NB, BLK), F32),
+            pltpu.VMEM((8, BLK), jnp.int32),
         ),
         in_specs=[hbm] * 9,
-        out_specs=(vmem, vmem, vmem),
+        out_specs=(vmem,) * 5,
         scratch_shapes=[
             pltpu.VMEM((NB, C, BLK), BF),
             pltpu.VMEM((3, NB, BLK), BF),
@@ -509,7 +527,6 @@
             pltpu.VMEM((TAPS, C, C), BF),
             pltpu.VMEM((1, C), BF),
             pltpu.VMEM((NB, BLK), F32),
-            pltpu.VMEM((8, BLK), jnp.int32),
             pltpu.SMEM((8, BLK), jnp.int32),
             pltpu.VMEM((NB, 8, BLK), F32),
             dma((10,)),
@@ -527,28 +544,39 @@
             pltpu.VMEM((COLS, NZ), F32),
             pltpu.VMEM((COLS * C, NZ), BF),
             pltpu.VMEM((GX, 8, BLK), F32),
-            pltpu.VMEM((GX, 8, BLK), F32),
             pltpu.VMEM((GX, CAP, C, BLK), BF),
-            pltpu.VMEM((GX * CAP, C, BLK), BF),
             pltpu.VMEM((GX, 8, 128), F32),
             pltpu.VMEM((GX, 8, 128), F32),
             pltpu.VMEM((GY, 8, 128), F32),
-            pltpu.VMEM((GX, 8, 128), F32),
             dma((GX,)), dma((GX,)), dma((8,)), dma((8,)), dma((8,)), dma((8,)),
             dma((GX,)), dma((GX,)), dma((GX,)), dma((GX,)), dma((GX,)), dma((GX,)),
             dma((GY,)), dma((GY,)), dma((GX,)), dma((GX,)),
         ],
         compiler_params=pltpu.CompilerParams(
-            collective_id=0, has_side_effects=True, vmem_limit_bytes=63 * 1024 * 1024
+            collective_id=0, has_side_effects=True, vmem_limit_bytes=40 * 1024 * 1024
         ),
         cost_estimate=pl.CostEstimate(
             flops=8_000_000_000, bytes_accessed=2_000_000, transcendentals=1_000_000
         ),
-    )(
-        point_feats, jnp.transpose(point_offsets, (1, 0, 2)), base_cells,
-        block_owners.reshape(1, NB), point_counts.reshape(1, 1), lift_weight, conv_weight,
-        read_weight.reshape(1, C), cotangent,
-    )
+    )(*(x if x.size == 1 else pltpu.with_memory_space_constraint(x, pltpu.HBM) for x in inputs))
+    return pl.pallas_call(
+        finish_kernel,
+        out_shape=(
+            jax.ShapeDtypeStruct((NB, BLK), F32),
+            jax.ShapeDtypeStruct((NB, C, BLK), BF),
+            jax.ShapeDtypeStruct((TAPS, C, C), F32),
+        ),
+        in_specs=[vmem] * 5,
+        out_specs=(hbm,) * 3,
+        scratch_shapes=[
+            pltpu.SMEM((8, BLK), jnp.int32),
+            pltpu.VMEM((NB, BLK), F32),
+            pltpu.VMEM((NB, C, BLK), BF),
+            pltpu.VMEM((TAPS, C, C), F32),
+            dma((7,)),
+        ],
+        compiler_params=pltpu.CompilerParams(vmem_limit_bytes=8 * 1024 * 1024),
+    )(*(pltpu.with_memory_space_constraint(x, pltpu.VMEM) for x in parts))
 
 
 def solution(mesh):

time: 60.8 us -> 54.8 us (0.901)
  local copies, waits for them, and re-layouts: 3.81 us -> 0 us
  Pallas kernels: 55.5 us -> 53.4 us
    unnamed x5 -> x0, local copies, waits for them, and re-layouts: 3.81 us -> none
    pallas_call x1 -> x2, Pallas kernels: 55.5 us -> 53.4 us  [the longest x1 51.5 us: local(): pl.pallas_call(kernel, out_shape=(pltpu.VMEM((GX * CAP, C, BLK), BF), plt...]
where the time goes in v3:
time: 54.8 us; the launch traced here: 54.7 us
  Pallas kernels  53.4 us (97%)
  between operations  1.29 us (2%)
    pallas_call x1, Pallas kernels, local(): pl.pallas_call(kernel, out_shape=(pltpu.VMEM((GX * CAP, C, BLK), BF), plt...  51.5 us
    pallas_call x1, Pallas kernels, local(): pl.pallas_call(finish_kernel, out_shape=(jax.ShapeDtypeStruct((NB, BLK),...  1.93 us

profile of v3, /device:TPU:1, one launch (start us, length us, event | category | flops | bytes accessed | tf_op | source)
XLA Modules:
  0.0 54.7 jit_solution(11541195861784381988)
XLA Ops:
  1.3 51.5 %shard_map.112 = (bf16[64,32,128]{2,1,0:T(8,128)(2,1)S(1)}, f32[32,8,128]{2,1,0:T(8,128)S(1)}, f32[32,8,128]{2,1,0:T(8,128)S(1)}, f32[32,128]{1,0:T(8,128)S(1)}, s32[8,128]{1,0:T(8,128)S(1)}) custom-call(bf16[32,32,128]{2,1,0:T(8,128)(2,1)} %feats_hbm.1, bf16[3,32,128]{2,1,0:T(8,128)(2,1)} %bitcast.5, s32[32,128]{1,0:T(8,128)} %base_hbm.1, s32[1,32]{1,0:T(1,128)} %bitcast.6, ...), custom_call_target="tpu_custom_call" | custom-call | flops 8000000000 | bytes 2000000 | tf_op jit(solution)/shard_map/pallas_call | solution.py:509
  52.7 1.9 %shard_map.113 = (f32[32,128]{1,0:T(8,128)}, bf16[32,32,128]{2,1,0:T(8,128)(2,1)}, f32[27,32,32]{2,1,0:T(8,128)}) custom-call(bf16[64,32,128]{2,1,0:T(8,128)(2,1)S(1)} %get-tuple-element.8.gfr, f32[32,8,128]{2,1,0:T(8,128)S(1)} %get-tuple-element.9.predr, f32[32,8,128]{2,1,0:T(8,128)S(1)} %get-tuple-element.10.red3, f32[32,128]{1,0:T(8,128)S(1)} %get-tuple-element.11.alive, ...), custom_call_target="tpu_custom_call" | custom-call | tf_op jit(solution)/shard_map/pallas_call | solution.py:562

commit v4 on v3

--- a/solution.py
+++ b/solution.py
@@ -27,6 +27,19 @@
 F32 = jnp.float32
 
 
+def partner(mx, n, sign):
+    m, dc = n // 2, lax.rem(n, 2)
+    dx, dz = lax.rem(m, 4), lax.rem(m // 4 + m, 4)
+    if sign < 0:
+        dx, dz = 4 - dx, 4 - dz
+    x, z, c = mx // 8, lax.rem(mx // 2, 4), lax.rem(mx, 2)
+    return lax.rem(x + dx, 4) * 8 + lax.rem(z + dz, 4) * 2 + lax.rem(c + dc, 2)
+
+
+def whole(ref, sem):
+    pltpu.make_async_copy(ref, ref, sem).wait()
+
+
 def dot(a, b, ca=1, cb=0):
     return lax.dot_general(a, b, (((ca,), (cb,)), ((), ())), preferred_element_type=F32)
 
@@ -48,7 +61,7 @@
     feats_hbm, offsets_hbm, base_hbm, owners_hbm, count_hbm, lift_hbm, conv_hbm, read_hbm, cot_hbm,
     gfr, predr, red3, alive_out, table,
     feats, offsets, base, owners, count, lift, conv, read, cot, slots, aux, in_sem, send, recv, acc, zs, planes, latp, gp, gs, wf, wb,
-    gout, field, gl, predmsg, gfs, redsrc, red1, red2,
+    gout, field, gl, predmsg, held, gfs, redsrc, red1, red2,
     s_send, s_recv, h_send, h_recv, i_send, i_recv, p_send, p_recv,
     f_send, f_recv, a_send, a_recv, b_send, b_recv, c_send, c_recv,
 ):
@@ -77,9 +90,6 @@
 
     for k in range(1, GY):
         pl.semaphore_signal(barrier, inc=1, device_id=(mx, lax.rem(my + k, GY)), device_id_type=MESH)
-    for px in (left, right):
-        for py in (down, up):
-            pl.semaphore_signal(barrier, inc=1, device_id=(px, py), device_id_type=MESH)
 
     fetched["owners"].wait()
     named = owners[...]
@@ -109,7 +119,14 @@
     tile_rows += [cell_y, cells - cell_y * (NZ - 1.0), high, grad - high, alive]
     for n, value in enumerate(tile_rows):
         aux[:, n, :] = value
-    fetched["feats"].wait()
+    for name in ("lift", "feats"):
+        fetched[name].wait()
+    lift_w = lift[...]
+    for part in range(4):
+        raw = jnp.concatenate([feats[8 * part + n] for n in range(8)], axis=1)
+        lifted = dot(lift_w, raw, 0, 0).astype(BF)
+        for n in range(8):
+            feats[8 * part + n] = lifted[:, n * BLK : (n + 1) * BLK]
     to_slots.wait()
 
     def place(o):
@@ -124,31 +141,30 @@
         send[o, CAP * C : CAP * C + 16, :] = jnp.concatenate(tails, axis=0).astype(BF)
 
     def points_copy(k):
-        to = lax.rem(mx + k, GX)
+        to = partner(mx, k, 1)
         return pltpu.make_async_remote_copy(
             src_ref=send.at[to], dst_ref=recv.at[mx],
-            send_sem=s_send.at[k], recv_sem=s_recv.at[k],
+            send_sem=s_send, recv_sem=s_recv.at[k // GROUP],
             device_id=(to, my), device_id_type=MESH,
         )
 
-    pl.semaphore_wait(barrier, GX - 1 + GY - 1 + 4)
+    pl.semaphore_wait(barrier, GX - 1 + GY - 1)
 
     @pl.loop(1, GX)
     def _(k):
-        place(lax.rem(mx + k, GX))
+        place(partner(mx, k, 1))
         points_copy(k).start()
 
     place(mx)
     recv[mx] = send[mx]
 
-    for name in ("lift", "conv", "read"):
+    for name in ("conv", "read"):
         fetched[name].wait()
     eye = jnp.where(
         lax.broadcasted_iota(jnp.int32, (C, C), 0) == lax.broadcasted_iota(jnp.int32, (C, C), 1),
         1.0, 0.0,
     )
     read_col = dot((eye * read[...].astype(F32)).astype(BF), jnp.ones((C, NZ), BF))
-    lift_w = lift[...]
 
     sub_z = lax.broadcasted_iota(jnp.int32, (NZ, WIDE), 0).astype(F32)
     sub_y = lax.broadcasted_iota(jnp.int32, (CY, WIDE), 0).astype(F32)
@@ -157,18 +173,17 @@
     @pl.loop(0, GROUPS)
     def _(g):
         blocks, tails = [], []
+
+        @pl.when(g == 0)
+        def _():
+            whole(recv.at[0 : GROUP - 1], s_recv.at[0])
+
+        @pl.when(g > 0)
+        def _():
+            whole(recv.at[0:GROUP], s_recv.at[g])
+
         for n in range(GROUP):
-            k = GROUP * g + n
-            if n == 0:
-
-                @pl.when(g > 0)
-                def _():
-                    points_copy(GROUP * g).wait_recv()
-
-            else:
-                points_copy(k).wait_recv()
-        for n in range(GROUP):
-            msg = recv[lax.rem(mx - (GROUP * g + n) + GX, GX)]
+            msg = recv[partner(mx, GROUP * g + n, -1)]
             blocks += [msg[0:C], msg[C : 2 * C]]
             tail = msg[2 * C : 2 * C + 16].astype(F32)
             tails += [tail[0:8], tail[8:16]]
@@ -185,7 +200,7 @@
         z = jnp.where(sub_z == at_z, near[2:3], jnp.where(sub_z == at_z + 1.0, far[2:3], 0.0))
         z = z.astype(BF)
         zs[g] = z
-        lifted = dot(lift_w, block, 0, 0).astype(BF).astype(F32)
+        lifted = block.astype(F32)
         rows = [
             (lifted * plane[x][y : y + 1]).astype(BF) for y in range(CY) for x in range(CX)
         ]
@@ -205,7 +220,7 @@
         )
         return [
             pltpu.make_async_remote_copy(
-                src_ref=src, dst_ref=dst, send_sem=sends.at[n], recv_sem=recvs.at[n],
+                src_ref=src, dst_ref=dst, send_sem=sends, recv_sem=recvs,
                 device_id=(px, py), device_id_type=MESH,
             )
             for n, (px, py, src, dst) in enumerate(ends)
@@ -259,10 +274,7 @@
                     lane = (yo + dy) * 128
                     wf[row : row + C, lane : lane + 128] = tile_f
                     wb[row : row + C, lane : lane + 128] = tile_b
-    for copy in halos:
-        copy.wait_recv()
-    for copy in halos:
-        copy.wait_send()
+    whole(latp.at[0:6], h_recv)
     clear_ends(latp)
 
     for pair in range(4):
@@ -320,10 +332,10 @@
     redsrc[TAPS:GX] = jnp.zeros((GX - TAPS, 8, 128), F32)
 
     def taps_copy(k):
-        to = lax.rem(mx + k, GX)
+        to = partner(mx, k, 1)
         return pltpu.make_async_remote_copy(
             src_ref=redsrc.at[to], dst_ref=red1.at[mx],
-            send_sem=a_send.at[k], recv_sem=a_recv.at[k],
+            send_sem=a_send, recv_sem=a_recv,
             device_id=(to, my), device_id_type=MESH,
         )
 
@@ -337,10 +349,10 @@
     scalars = jnp.concatenate([scalar_hi, scalar_lo], axis=0)
 
     def pred_copy(k):
-        to = lax.rem(mx - k + GX, GX)
+        to = partner(mx, k, -1)
         return pltpu.make_async_remote_copy(
             src_ref=predmsg.at[k, 0:CAP], dst_ref=predr.at[mx, 0:CAP],
-            send_sem=p_send.at[k], recv_sem=p_recv.at[k],
+            send_sem=p_send, recv_sem=p_recv,
             device_id=(to, my), device_id_type=MESH,
         )
 
@@ -364,10 +376,7 @@
 
     predr[mx, 0:CAP, :] = predmsg[0, 0:CAP, :]
 
-    for copy in halos2:
-        copy.wait_recv()
-    for copy in halos2:
-        copy.wait_send()
+    whole(gp.at[0:6], i_recv)
     clear_ends(gp)
     for pair in range(4):
         back = conv_pair(wb, gp, pair)
@@ -376,71 +385,72 @@
         ).astype(BF)
 
     def feats_copy(k):
-        to = lax.rem(mx - k + GX, GX)
+        to = partner(mx, k, -1)
         return pltpu.make_async_remote_copy(
             src_ref=gfs.at[k], dst_ref=gfr.at[pl.ds(CAP * mx, CAP)],
-            send_sem=f_send.at[k], recv_sem=f_recv.at[k],
+            send_sem=f_send, recv_sem=f_recv,
             device_id=(to, my), device_id_type=MESH,
         )
 
     def rows_copy(k):
         return pltpu.make_async_remote_copy(
             src_ref=red2.at[my], dst_ref=red2.at[my],
-            send_sem=b_send.at[k], recv_sem=b_recv.at[k],
+            send_sem=b_send, recv_sem=b_recv,
             device_id=(mx, lax.rem(my + k, GY)), device_id_type=MESH,
         )
 
-    def send_back(g):
+    def collect(g):
         got = dot(gl[...], zs[g])
         total = jnp.zeros((C, WIDE), F32)
         for y in range(CY):
             for x in range(CX):
                 n = (y * CX + x) * C
                 total = total + got[n : n + C] * planes[g, x * CY + y : x * CY + y + 1, :]
-        back = dot(lift_w, total.astype(BF)).astype(BF)
+        return total.astype(BF)
+
+    def finish(g, total):
+        back = dot(lift_w, total).astype(BF)
         for n in range(GROUP):
-            k = GROUP * g + n
             for r in range(CAP):
                 lane = n * PTS + r * BLK
-                gfs[k, r] = back[:, lane : lane + BLK]
-            if n == 0:
-
-                @pl.when(g > 0)
-                def _():
-                    feats_copy(GROUP * g).start()
-
-            else:
-                feats_copy(k).start()
-
-    @pl.loop(1, 4)
+                gfs[GROUP * g + n, r] = back[:, lane : lane + BLK]
+
+    def send_back(g):
+        for n in range(GROUP):
+            feats_copy(GROUP * g + n).start()
+
+    def step(g):
+        before = held[...]
+        total = collect(g)
+        finish(g - 1, before)
+        held[...] = total
+        send_back(g - 1)
+
+    held[...] = collect(1)
+
+    @pl.loop(2, 4)
     def _(g):
-        send_back(g)
+        step(g)
 
     red1[mx] = redsrc[mx]
 
-    @pl.loop(1, GX)
-    def _(k):
-        taps_copy(k).wait_recv()
-
+    whole(red1.at[0 : GX - 1], a_recv)
     red2[my] = jnp.sum(red1[...], axis=0)
     for k in range(1, GY):
         rows_copy(k).start()
 
     @pl.loop(4, GROUPS)
     def _(g):
-        send_back(g)
-
-    for k in range(1, GY):
-        rows_copy(k).wait_recv()
-    for k in range(1, GY):
-        rows_copy(k).wait_send()
+        step(g)
+
+    whole(red2.at[0 : GY - 1], b_recv)
     red3[mx] = (red2[0] + red2[1] + red2[2] + red2[3]) * (1.0 / GX)
 
     def total_copy(k):
-        to = lax.rem(mx + k, GX)
+        to = partner(mx, k, 1)
         return pltpu.make_async_remote_copy(
             src_ref=red3.at[mx], dst_ref=red3.at[mx],
-            send_sem=c_send.at[k], recv_sem=c_recv.at[k],
+            send_sem=c_send, recv_sem=c_recv,
             device_id=(to, my), device_id_type=MESH,
         )
 
@@ -448,16 +458,25 @@
     def _(k):
         total_copy(k).start()
 
-    send_back(0)
+    before = held[...]
+    total = collect(0)
+    finish(GROUPS - 1, before)
+    send_back(GROUPS - 1)
+    finish(0, total)
+    for n in range(1, GROUP):
+        feats_copy(n).start()
     gfr[pl.ds(CAP * mx, CAP)] = gfs[0]
 
-    @pl.loop(1, GX)
-    def _(k):
-        pred_copy(k).wait()
-        total_copy(k).wait()
-        feats_copy(k).wait()
-        points_copy(k).wait_send()
-        taps_copy(k).wait_send()
+    for sem in (p_recv, p_send):
+        whole(predr.at[0 : GX - 1, 0:CAP], sem)
+    for sem in (c_recv, c_send, a_send):
+        whole(red3.at[0 : GX - 1], sem)
+    for sem in (f_recv, f_send):
+        whole(gfr.at[0 : CAP * (GX - 1)], sem)
+    whole(red2.at[0 : GY - 1], b_send)
+    whole(latp.at[0:6], h_send)
+    whole(gp.at[0:6], i_send)
+    whole(recv.at[0 : GX - 1], s_send)
 
 
 def finish_kernel(
@@ -544,13 +563,12 @@
             pltpu.VMEM((COLS, NZ), F32),
             pltpu.VMEM((COLS * C, NZ), BF),
             pltpu.VMEM((GX, 8, BLK), F32),
+            pltpu.VMEM((C, WIDE), BF),
             pltpu.VMEM((GX, CAP, C, BLK), BF),
             pltpu.VMEM((GX, 8, 128), F32),
             pltpu.VMEM((GX, 8, 128), F32),
             pltpu.VMEM((GY, 8, 128), F32),
-            dma((GX,)), dma((GX,)), dma((8,)), dma((8,)), dma((8,)), dma((8,)),
-            dma((GX,)), dma((GX,)), dma((GX,)), dma((GX,)), dma((GX,)), dma((GX,)),
-            dma((GY,)), dma((GY,)), dma((GX,)), dma((GX,)),
+            dma, dma((GROUPS,)), dma, dma, dma, dma, dma, dma, dma, dma, dma, dma, dma, dma, dma, dma,
         ],
         compiler_params=pltpu.CompilerParams(
             collective_id=0, has_side_effects=True, vmem_limit_bytes=40 * 1024 * 1024

time: 54.8 us -> 47.7 us (0.87)
  Pallas kernels: 53.4 us -> 46.3 us
    pallas_call x1, Pallas kernels: 51.5 us -> 44.3 us  [local(): pl.pallas_call(kernel, out_shape=(pltpu.VMEM((GX * CAP, C, BLK), BF), plt...]
where the time goes in v4:
time: 47.7 us; the launch traced here: 47.6 us
  Pallas kernels  46.3 us (97%)
  between operations  1.29 us (3%)
    pallas_call x1, Pallas kernels, local(): pl.pallas_call(kernel, out_shape=(pltpu.VMEM((GX * CAP, C, BLK), BF), plt...  44.3 us
    pallas_call x1, Pallas kernels, local(): pl.pallas_call(finish_kernel, out_shape=(jax.ShapeDtypeStruct((NB, BLK),...  1.93 us

profile of v4, /device:TPU:1, one launch (start us, length us, event | category | flops | bytes accessed | tf_op | source)
XLA Modules:
  0.0 47.6 jit_solution(5293941863382219382)
XLA Ops:
  1.3 44.3 %shard_map.112 = (bf16[64,32,128]{2,1,0:T(8,128)(2,1)S(1)}, f32[32,8,128]{2,1,0:T(8,128)S(1)}, f32[32,8,128]{2,1,0:T(8,128)S(1)}, f32[32,128]{1,0:T(8,128)S(1)}, s32[8,128]{1,0:T(8,128)S(1)}) custom-call(bf16[32,32,128]{2,1,0:T(8,128)(2,1)} %feats_hbm.1, bf16[3,32,128]{2,1,0:T(8,128)(2,1)} %bitcast.5, s32[32,128]{1,0:T(8,128)} %base_hbm.1, s32[1,32]{1,0:T(1,128)} %bitcast.6, ...), custom_call_target="tpu_custom_call" | custom-call | flops 8000000000 | bytes 2000000 | tf_op jit(solution)/shard_map/pallas_call | solution.py:528
  45.6 1.9 %shard_map.113 = (f32[32,128]{1,0:T(8,128)}, bf16[32,32,128]{2,1,0:T(8,128)(2,1)}, f32[27,32,32]{2,1,0:T(8,128)}) custom-call(bf16[64,32,128]{2,1,0:T(8,128)(2,1)S(1)} %get-tuple-element.8.gfr, f32[32,8,128]{2,1,0:T(8,128)S(1)} %get-tuple-element.9.predr, f32[32,8,128]{2,1,0:T(8,128)S(1)} %get-tuple-element.10.red3, f32[32,128]{1,0:T(8,128)S(1)} %get-tuple-element.11.alive, ...), custom_call_target="tpu_custom_call" | custom-call | tf_op jit(solution)/shard_map/pallas_call | solution.py:580

commit v5 on v4

--- a/solution.py
+++ b/solution.py
@@ -28,12 +28,12 @@
 
 
 def partner(mx, n, sign):
-    m, dc = n // 2, lax.rem(n, 2)
-    dx, dz = lax.rem(m, 4), lax.rem(m // 4 + m, 4)
-    if sign < 0:
-        dx, dz = 4 - dx, 4 - dz
-    x, z, c = mx // 8, lax.rem(mx // 2, 4), lax.rem(mx, 2)
-    return lax.rem(x + dx, 4) * 8 + lax.rem(z + dz, 4) * 2 + lax.rem(c + dc, 2)
+    return lax.rem(mx + sign * lax.rem(11 * n, GX) + GX, GX)
+
+
+def snake(index):
+    x, z, core = index // 8, lax.rem(index // 2, 4), lax.rem(index, 2)
+    return x * 8 + (z + lax.rem(x, 2) * (3 - 2 * z)) * 2 + core
 
 
 def whole(ref, sem):
@@ -67,7 +67,8 @@
 ):
     mx = lax.axis_index("gx")
     my = lax.axis_index("gy")
-    right, left = lax.rem(mx + 1, GX), lax.rem(mx + GX - 1, GX)
+    slab = snake(mx)
+    right, left = snake(lax.rem(slab + 1, GX)), snake(lax.rem(slab + GX - 1, GX))
     up, down = lax.rem(my + 1, GY), lax.rem(my + GY - 1, GY)
 
     pairs = {
@@ -129,16 +130,17 @@
             feats[8 * part + n] = lifted[:, n * BLK : (n + 1) * BLK]
     to_slots.wait()
 
-    def place(o):
+    def place(to):
+        o = snake(to)
         tails = []
         for r in range(CAP):
             j = slots[0, CAP * o + r]
             jj = jnp.maximum(j, 0)
             here = jnp.where(j >= 0, 1.0, 0.0)
             tail = aux[jj] * here
-            send[o, r * C : (r + 1) * C, :] = (feats[jj].astype(F32) * tail[7:8]).astype(BF)
+            send[to, r * C : (r + 1) * C, :] = (feats[jj].astype(F32) * tail[7:8]).astype(BF)
             tails.append(tail)
-        send[o, CAP * C : CAP * C + 16, :] = jnp.concatenate(tails, axis=0).astype(BF)
+        send[to, CAP * C : CAP * C + 16, :] = jnp.concatenate(tails, axis=0).astype(BF)
 
     def points_copy(k):
         to = partner(mx, k, 1)
@@ -209,14 +211,14 @@
 
     def halo_copies(buf, sends, recvs):
         ends = (
-            (right, my, buf.at[1:9, 2], buf.at[1:9, 0]),
-            (left, my, buf.at[1:9, 1], buf.at[1:9, 3]),
-            (mx, up, buf.at[8, 1:3], buf.at[0, 1:3]),
-            (mx, down, buf.at[1, 1:3], buf.at[9, 1:3]),
             (right, up, buf.at[8, 2], buf.at[0, 0]),
             (right, down, buf.at[1, 2], buf.at[9, 0]),
             (left, up, buf.at[8, 1], buf.at[0, 3]),
             (left, down, buf.at[1, 1], buf.at[9, 3]),
+            (mx, up, buf.at[8, 1:3], buf.at[0, 1:3]),
+            (mx, down, buf.at[1, 1:3], buf.at[9, 1:3]),
+            (right, my, buf.at[1:9, 2], buf.at[1:9, 0]),
+            (left, my, buf.at[1:9, 1], buf.at[1:9, 3]),
         )
         return [
             pltpu.make_async_remote_copy(
@@ -227,11 +229,11 @@
         ]
 
     def clear_ends(buf):
-        @pl.when(mx == 0)
+        @pl.when(slab == 0)
         def _():
             buf[:, 0] = jnp.zeros((10, C, NZ), BF)
 
-        @pl.when(mx == GX - 1)
+        @pl.when(slab == GX - 1)
         def _():
             buf[:, 3] = jnp.zeros((10, C, NZ), BF)
 
@@ -351,7 +353,7 @@
     def pred_copy(k):
         to = partner(mx, k, -1)
         return pltpu.make_async_remote_copy(
-            src_ref=predmsg.at[k, 0:CAP], dst_ref=predr.at[mx, 0:CAP],
+            src_ref=predmsg.at[k, 0:CAP], dst_ref=predr.at[slab, 0:CAP],
             send_sem=p_send, recv_sem=p_recv,
             device_id=(to, my), device_id_type=MESH,
         )
@@ -374,7 +376,7 @@
             else:
                 pred_copy(k).start()
 
-    predr[mx, 0:CAP, :] = predmsg[0, 0:CAP, :]
+    predr[slab, 0:CAP, :] = predmsg[0, 0:CAP, :]
 
     whole(gp.at[0:6], i_recv)
     clear_ends(gp)
@@ -387,7 +389,7 @@
     def feats_copy(k):
         to = partner(mx, k, -1)
         return pltpu.make_async_remote_copy(
-            src_ref=gfs.at[k], dst_ref=gfr.at[pl.ds(CAP * mx, CAP)],
+            src_ref=gfs.at[k], dst_ref=gfr.at[pl.ds(CAP * slab, CAP)],
             send_sem=f_send, recv_sem=f_recv,
             device_id=(to, my), device_id_type=MESH,
         )
@@ -465,7 +467,7 @@
     finish(0, total)
     for n in range(1, GROUP):
         feats_copy(n).start()
-    gfr[pl.ds(CAP * mx, CAP)] = gfs[0]
+    gfr[pl.ds(CAP * slab, CAP)] = gfs[0]
 
     for sem in (p_recv, p_send):
         whole(predr.at[0 : GX - 1, 0:CAP], sem)

time: 47.7 us -> 46.9 us (0.983)
  Pallas kernels: 46.3 us -> 45.5 us
    pallas_call x1, Pallas kernels: 44.3 us -> 43.5 us  [local(): pl.pallas_call(kernel, out_shape=(pltpu.VMEM((GX * CAP, C, BLK), BF), plt...]
where the time goes in v5:
time: 46.9 us; the launch traced here: 46.8 us
  Pallas kernels  45.5 us (97%)
  between operations  1.29 us (3%)
    pallas_call x1, Pallas kernels, local(): pl.pallas_call(kernel, out_shape=(pltpu.VMEM((GX * CAP, C, BLK), BF), plt...  43.5 us
    pallas_call x1, Pallas kernels, local(): pl.pallas_call(finish_kernel, out_shape=(jax.ShapeDtypeStruct((NB, BLK),...  1.93 us

profile of v5, /device:TPU:1, one launch (start us, length us, event | category | flops | bytes accessed | tf_op | source)
XLA Modules:
  0.0 46.8 jit_solution(4278793378392547732)
XLA Ops:
  1.3 43.5 %shard_map.112 = (bf16[64,32,128]{2,1,0:T(8,128)(2,1)S(1)}, f32[32,8,128]{2,1,0:T(8,128)S(1)}, f32[32,8,128]{2,1,0:T(8,128)S(1)}, f32[32,128]{1,0:T(8,128)S(1)}, s32[8,128]{1,0:T(8,128)S(1)}) custom-call(bf16[32,32,128]{2,1,0:T(8,128)(2,1)} %feats_hbm.1, bf16[3,32,128]{2,1,0:T(8,128)(2,1)} %bitcast.5, s32[32,128]{1,0:T(8,128)} %base_hbm.1, s32[1,32]{1,0:T(1,128)} %bitcast.6, ...), custom_call_target="tpu_custom_call" | custom-call | flops 8000000000 | bytes 2000000 | tf_op jit(solution)/shard_map/pallas_call | solution.py:530
  44.8 1.9 %shard_map.113 = (f32[32,128]{1,0:T(8,128)}, bf16[32,32,128]{2,1,0:T(8,128)(2,1)}, f32[27,32,32]{2,1,0:T(8,128)}) custom-call(bf16[64,32,128]{2,1,0:T(8,128)(2,1)S(1)} %get-tuple-element.8.gfr, f32[32,8,128]{2,1,0:T(8,128)S(1)} %get-tuple-element.9.predr, f32[32,8,128]{2,1,0:T(8,128)S(1)} %get-tuple-element.10.red3, f32[32,128]{1,0:T(8,128)S(1)} %get-tuple-element.11.alive, ...), custom_call_target="tpu_custom_call" | custom-call | tf_op jit(solution)/shard_map/pallas_call | solution.py:582

commit v6 on v5

--- a/solution.py
+++ b/solution.py
@@ -59,8 +59,8 @@
 
 def kernel(
     feats_hbm, offsets_hbm, base_hbm, owners_hbm, count_hbm, lift_hbm, conv_hbm, read_hbm, cot_hbm,
-    gfr, predr, red3, alive_out, table,
-    feats, offsets, base, owners, count, lift, conv, read, cot, slots, aux, in_sem, send, recv, acc, zs, planes, latp, gp, gs, wf, wb,
+    pred_out, feats_out, conv_out,
+    feats, offsets, base, owners, count, lift, conv, read, cot, table, slots, aux, gfr, predr, red3, in_sem, send, recv, acc, zs, planes, latp, gp, gs, wf, wb,
     gout, field, gl, predmsg, held, gfs, redsrc, red1, red2,
     s_send, s_recv, h_send, h_recv, i_send, i_recv, p_send, p_recv,
     f_send, f_recv, a_send, a_recv, b_send, b_recv, c_send, c_recv,
@@ -113,7 +113,6 @@
     cells = base[...].astype(F32)
     cell_y = jnp.floor((cells + 0.5) * (1.0 / (NZ - 1)))
     alive = jnp.where(rows * BLK + lanes < count[...], 1.0, 0.0)
-    alive_out[...] = alive
     grad = cot[...] * alive
     high = grad.astype(BF).astype(F32)
     tile_rows = [offsets[n].astype(F32) for n in range(3)]
@@ -310,10 +309,11 @@
     for copy in halos2:
         copy.start()
 
-    tap = jnp.zeros((4 * 4 * C, 3 * 128), F32)
-    for pair in range(4):
-        window = latp[2 * pair : 2 * pair + 4].reshape(4 * 4 * C, NZ)
-        tap = tap + dot(window, gs[pair], 1, 1)
+    windows = [latp[2 * pair : 2 * pair + 4].reshape(4 * 4 * C, NZ) for pair in range(4)]
+    tap = dot(
+        jnp.concatenate(windows, axis=1),
+        jnp.concatenate([gs[pair] for pair in range(4)], axis=1), 1, 1,
+    )
     quarter = lax.broadcasted_iota(jnp.int32, (C, 128), 1) // C
     quarter8 = lax.broadcasted_iota(jnp.int32, (8, 128), 1) // C
     for dx in range(3):
@@ -430,7 +430,7 @@
 
     held[...] = collect(1)
 
-    @pl.loop(2, 4)
+    @pl.loop(2, 5)
     def _(g):
         step(g)
 
@@ -441,24 +441,9 @@
     for k in range(1, GY):
         rows_copy(k).start()
 
-    @pl.loop(4, GROUPS)
+    @pl.loop(5, GROUPS)
     def _(g):
         step(g)
-
-    whole(red2.at[0 : GY - 1], b_recv)
-    red3[mx] = (red2[0] + red2[1] + red2[2] + red2[3]) * (1.0 / GX)
-
-    def total_copy(k):
-        to = partner(mx, k, 1)
-        return pltpu.make_async_remote_copy(
-            src_ref=red3.at[mx], dst_ref=red3.at[mx],
-            send_sem=c_send, recv_sem=c_recv,
-            device_id=(to, my), device_id_type=MESH,
-        )
-
-    @pl.loop(1, GX)
-    def _(k):
-        total_copy(k).start()
 
     before = held[...]
     total = collect(0)
@@ -469,48 +454,57 @@
         feats_copy(n).start()
     gfr[pl.ds(CAP * slab, CAP)] = gfs[0]
 
-    for sem in (p_recv, p_send):
-        whole(predr.at[0 : GX - 1, 0:CAP], sem)
-    for sem in (c_recv, c_send, a_send):
+    whole(red2.at[0 : GY - 1], b_recv)
+    red3[mx] = (red2[0] + red2[1] + red2[2] + red2[3]) * (1.0 / GX)
+
+    def total_copy(k):
+        to = partner(mx, k, 1)
+        return pltpu.make_async_remote_copy(
+            src_ref=red3.at[mx], dst_ref=red3.at[mx],
+            send_sem=c_send, recv_sem=c_recv,
+            device_id=(to, my), device_id_type=MESH,
+        )
+
+    @pl.loop(1, GX)
+    def _(k):
+        total_copy(k).start()
+
+    whole(predr.at[0 : GX - 1, 0:CAP], p_recv)
+    whole(gfr.at[0 : CAP * (GX - 1)], f_recv)
+
+    @pl.loop(0, NB)
+    def _(j):
+        s = slots[1, j]
+        keep = aux[j, 7:8, :]
+        feats_out[j] = (gfr[s].astype(F32) * keep).astype(BF)
+        both = predr[s // CAP]
+        value = jnp.where(lax.rem(s, CAP) == 0, both[0:1], both[1:2])
+        pred_out[pl.ds(j, 1), :] = value * keep
+
+    whole(red3.at[0 : GX - 1], c_recv)
+    for d in range(TAPS):
+        packed = red3[d]
+        for q in range(4):
+            piece = packed if q == 0 else pltpu.roll(packed, 128 - C * q, 1)
+            conv_out[d, 8 * q : 8 * q + 8, :] = piece[:, 0:C]
+
+    whole(predr.at[0 : GX - 1, 0:CAP], p_send)
+    whole(gfr.at[0 : CAP * (GX - 1)], f_send)
+    for sem in (c_send, a_send):
         whole(red3.at[0 : GX - 1], sem)
-    for sem in (f_recv, f_send):
-        whole(gfr.at[0 : CAP * (GX - 1)], sem)
     whole(red2.at[0 : GY - 1], b_send)
     whole(latp.at[0:6], h_send)
     whole(gp.at[0:6], i_send)
     whole(recv.at[0 : GX - 1], s_send)
 
 
-def finish_kernel(
-    gfr, predr, red3, alive, table, pred_out, feats_out, conv_out,
-    slots, pred, feats, conv, sems,
-):
-    to_slots = pltpu.make_async_copy(table, slots, sems.at[0])
-    to_slots.start()
-    for d in range(TAPS):
-        packed = red3[d]
-        for q in range(4):
-            piece = packed if q == 0 else pltpu.roll(packed, 128 - C * q, 1)
-            conv[d, 8 * q : 8 * q + 8, :] = piece[:, 0:C]
-    copies = [pltpu.make_async_copy(conv, conv_out, sems.at[1])]
-    copies[0].start()
-    to_slots.wait()
-    for part in range(4):
-
-        @pl.loop(8 * part, 8 * part + 8)
-        def _(j):
-            s = slots[1, j]
-            keep = alive[pl.ds(j, 1), :]
-            feats[j] = (gfr[s].astype(F32) * keep).astype(BF)
-            both = predr[s // CAP]
-            value = jnp.where(lax.rem(s, CAP) == 0, both[0:1], both[1:2])
-            pred[pl.ds(j, 1), :] = value * keep
-
-        span = pl.ds(8 * part, 8)
-        copies.append(pltpu.make_async_copy(feats.at[span], feats_out.at[span], sems.at[2 + part]))
-        copies[-1].start()
-    copies.append(pltpu.make_async_copy(pred, pred_out, sems.at[6]))
-    copies[-1].start()
+def finish_kernel(pred, feats, conv, pred_out, feats_out, conv_out, sems):
+    copies = [
+        pltpu.make_async_copy(src, dst, sems.at[n])
+        for n, (src, dst) in enumerate(((conv, conv_out), (feats, feats_out), (pred, pred_out)))
+    ]
+    for copy in copies:
+        copy.start()
     for copy in copies:
         copy.wait()
 
@@ -530,14 +524,12 @@
     parts = pl.pallas_call(
         kernel,
         out_shape=(
-            pltpu.VMEM((GX * CAP, C, BLK), BF),
-            pltpu.VMEM((GX, 8, BLK), F32),
-            pltpu.VMEM((GX, 8, 128), F32),
             pltpu.VMEM((NB, BLK), F32),
-            pltpu.VMEM((8, BLK), jnp.int32),
+            pltpu.VMEM((NB, C, BLK), BF),
+            pltpu.VMEM((TAPS, C, C), F32),
         ),
         in_specs=[hbm] * 9,
-        out_specs=(vmem,) * 5,
+        out_specs=(vmem,) * 3,
         scratch_shapes=[
             pltpu.VMEM((NB, C, BLK), BF),
             pltpu.VMEM((3, NB, BLK), BF),
@@ -548,8 +540,12 @@
             pltpu.VMEM((TAPS, C, C), BF),
             pltpu.VMEM((1, C), BF),
             pltpu.VMEM((NB, BLK), F32),
+            pltpu.VMEM((8, BLK), jnp.int32),
             pltpu.SMEM((8, BLK), jnp.int32),
             pltpu.VMEM((NB, 8, BLK), F32),
+            pltpu.VMEM((GX * CAP, C, BLK), BF),
+            pltpu.VMEM((GX, 8, BLK), F32),
+            pltpu.VMEM((GX, 8, 128), F32),
             dma((10,)),
             pltpu.VMEM((GX, CAP * C + 16, BLK), BF),
             pltpu.VMEM((GX, CAP * C + 16, BLK), BF),
@@ -586,15 +582,9 @@
             jax.ShapeDtypeStruct((NB, C, BLK), BF),
             jax.ShapeDtypeStruct((TAPS, C, C), F32),
         ),
-        in_specs=[vmem] * 5,
+        in_specs=[vmem] * 3,
         out_specs=(hbm,) * 3,
-        scratch_shapes=[
-            pltpu.SMEM((8, BLK), jnp.int32),
-            pltpu.VMEM((NB, BLK), F32),
-            pltpu.VMEM((NB, C, BLK), BF),
-            pltpu.VMEM((TAPS, C, C), F32),
-            dma((7,)),
-        ],
+        scratch_shapes=[dma((3,))],
         compiler_params=pltpu.CompilerParams(vmem_limit_bytes=8 * 1024 * 1024),
     )(*(pltpu.with_memory_space_constraint(x, pltpu.VMEM) for x in parts))
 

time: 46.9 us -> 46.1 us (0.983)
  Pallas kernels: 45.5 us -> 44.6 us
    pallas_call x1, Pallas kernels: 1.93 us -> 0.88 us  [local(): pl.pallas_call(finish_kernel, out_shape=(jax.ShapeDtypeStruct((NB, BLK),...]
where the time goes in v6:
time: 46.1 us; the launch traced here: 45.9 us
  Pallas kernels  44.6 us (97%)
  between operations  1.29 us (3%)
    pallas_call x1, Pallas kernels, local(): pl.pallas_call(kernel, out_shape=(pltpu.VMEM((NB, BLK), F32), pltpu.VMEM(...  43.8 us

profile of v6, /device:TPU:1, one launch (start us, length us, event | category | flops | bytes accessed | tf_op | source)
XLA Modules:
  0.0 45.9 jit_solution(4999901223888553359)
XLA Ops:
  1.3 43.8 %shard_map.112 = (f32[32,128]{1,0:T(8,128)S(1)}, bf16[32,32,128]{2,1,0:T(8,128)(2,1)S(1)}, f32[27,32,32]{2,1,0:T(8,128)S(1)}) custom-call(bf16[32,32,128]{2,1,0:T(8,128)(2,1)} %feats_hbm.1, bf16[3,32,128]{2,1,0:T(8,128)(2,1)} %bitcast.5, s32[32,128]{1,0:T(8,128)} %base_hbm.1, s32[1,32]{1,0:T(1,128)} %bitcast.6, s32[1,1]{1,0:T(1,128)} %bitcast.4.count_hbm, ...), custom_call_target="tpu_custom_call" | custom-call | flops 8000000000 | bytes 2000000 | tf_op jit(solution)/shard_map/pallas_call | solution.py:524
  45.0 0.9 %shard_map.113 = (f32[32,128]{1,0:T(8,128)}, bf16[32,32,128]{2,1,0:T(8,128)(2,1)}, f32[27,32,32]{2,1,0:T(8,128)}) custom-call(f32[32,128]{1,0:T(8,128)S(1)} %get-tuple-element.6.pred, bf16[32,32,128]{2,1,0:T(8,128)(2,1)S(1)} %get-tuple-element.7.feats, f32[27,32,32]{2,1,0:T(8,128)S(1)} %get-tuple-element.8.conv), custom_call_target="tpu_custom_call" | custom-call | tf_op jit(solution)/shard_map/pallas_call | solution.py:578

commit v7 on v6

--- a/solution.py
+++ b/solution.py
@@ -28,7 +28,7 @@
 
 
 def partner(mx, n, sign):
-    return lax.rem(mx + sign * lax.rem(11 * n, GX) + GX, GX)
+    return lax.rem(mx + sign * lax.rem(13 * n, GX) + GX, GX)
 
 
 def snake(index):

time: 46.1 us -> 45.2 us (0.980)
  Pallas kernels: 44.6 us -> 43.8 us
    pallas_call x1, Pallas kernels: 43.8 us -> 42.9 us  [local(): pl.pallas_call(kernel, out_shape=(pltpu.VMEM((NB, BLK), F32), pltpu.VMEM(...]
where the time goes in v7:
time: 45.2 us; the launch traced here: 45.1 us
  Pallas kernels  43.8 us (97%)
  between operations  1.29 us (3%)
    pallas_call x1, Pallas kernels, local(): pl.pallas_call(kernel, out_shape=(pltpu.VMEM((NB, BLK), F32), pltpu.VMEM(...  42.9 us

profile of v7, /device:TPU:1, one launch (start us, length us, event | category | flops | bytes accessed | tf_op | source)
XLA Modules:
  0.0 45.1 jit_solution(4137064199900094889)
XLA Ops:
  1.3 42.9 %shard_map.112 = (f32[32,128]{1,0:T(8,128)S(1)}, bf16[32,32,128]{2,1,0:T(8,128)(2,1)S(1)}, f32[27,32,32]{2,1,0:T(8,128)S(1)}) custom-call(bf16[32,32,128]{2,1,0:T(8,128)(2,1)} %feats_hbm.1, bf16[3,32,128]{2,1,0:T(8,128)(2,1)} %bitcast.5, s32[32,128]{1,0:T(8,128)} %base_hbm.1, s32[1,32]{1,0:T(1,128)} %bitcast.6, s32[1,1]{1,0:T(1,128)} %bitcast.4.count_hbm, ...), custom_call_target="tpu_custom_call" | custom-call | flops 8000000000 | bytes 2000000 | tf_op jit(solution)/shard_map/pallas_call | solution.py:524
  44.2 0.9 %shard_map.113 = (f32[32,128]{1,0:T(8,128)}, bf16[32,32,128]{2,1,0:T(8,128)(2,1)}, f32[27,32,32]{2,1,0:T(8,128)}) custom-call(f32[32,128]{1,0:T(8,128)S(1)} %get-tuple-element.6.pred, bf16[32,32,128]{2,1,0:T(8,128)(2,1)S(1)} %get-tuple-element.7.feats, f32[27,32,32]{2,1,0:T(8,128)S(1)} %get-tuple-element.8.conv), custom_call_target="tpu_custom_call" | custom-call | tf_op jit(solution)/shard_map/pallas_call | solution.py:578

commit v8 on v7

--- a/solution.py
+++ b/solution.py
@@ -417,6 +417,22 @@
                 lane = n * PTS + r * BLK
                 gfs[GROUP * g + n, r] = back[:, lane : lane + BLK]
 
+    def first_half(h):
+        span = slice(h * WIDE // 2, (h + 1) * WIDE // 2)
+        got = dot(gl[...], zs[1, :, span])
+        total = jnp.zeros((C, WIDE // 2), F32)
+        for y in range(CY):
+            for x in range(CX):
+                n = (y * CX + x) * C
+                total = total + got[n : n + C] * planes[1, x * CY + y : x * CY + y + 1, span]
+        back = dot(lift_w, total.astype(BF)).astype(BF)
+        for n in range(GROUP // 2):
+            k = GROUP + h * GROUP // 2 + n
+            for r in range(CAP):
+                lane = n * PTS + r * BLK
+                gfs[k, r] = back[:, lane : lane + BLK]
+            feats_copy(k).start()
+
     def send_back(g):
         for n in range(GROUP):
             feats_copy(GROUP * g + n).start()
@@ -428,9 +444,11 @@
         held[...] = total
         send_back(g - 1)
 
-    held[...] = collect(1)
-
-    @pl.loop(2, 5)
+    first_half(0)
+    first_half(1)
+    held[...] = collect(2)
+
+    @pl.loop(3, 5)
     def _(g):
         step(g)
 

time: 45.2 us -> 45.3 us (level)
  no operation moved by 1% of the time
where the time goes in v8:
time: 45.3 us; the launch traced here: 45.2 us
  Pallas kernels  43.9 us (97%)
  between operations  1.29 us (3%)
    pallas_call x1, Pallas kernels, local(): pl.pallas_call(kernel, out_shape=(pltpu.VMEM((NB, BLK), F32), pltpu.VMEM(...  43 us

profile of v8, /device:TPU:1, one launch (start us, length us, event | category | flops | bytes accessed | tf_op | source)
XLA Modules:
  0.0 45.2 jit_solution(3562122936078450879)
XLA Ops:
  1.3 43.0 %shard_map.112 = (f32[32,128]{1,0:T(8,128)S(1)}, bf16[32,32,128]{2,1,0:T(8,128)(2,1)S(1)}, f32[27,32,32]{2,1,0:T(8,128)S(1)}) custom-call(bf16[32,32,128]{2,1,0:T(8,128)(2,1)} %feats_hbm.1, bf16[3,32,128]{2,1,0:T(8,128)(2,1)} %bitcast.5, s32[32,128]{1,0:T(8,128)} %base_hbm.1, s32[1,32]{1,0:T(1,128)} %bitcast.6, s32[1,1]{1,0:T(1,128)} %bitcast.4.count_hbm, ...), custom_call_target="tpu_custom_call" | custom-call | flops 8000000000 | bytes 2000000 | tf_op jit(solution)/shard_map/pallas_call | solution.py:542
  44.3 0.9 %shard_map.113 = (f32[32,128]{1,0:T(8,128)}, bf16[32,32,128]{2,1,0:T(8,128)(2,1)}, f32[27,32,32]{2,1,0:T(8,128)}) custom-call(f32[32,128]{1,0:T(8,128)S(1)} %get-tuple-element.6.pred, bf16[32,32,128]{2,1,0:T(8,128)(2,1)S(1)} %get-tuple-element.7.feats, f32[27,32,32]{2,1,0:T(8,128)S(1)} %get-tuple-element.8.conv), custom_call_target="tpu_custom_call" | custom-call | tf_op jit(solution)/shard_map/pallas_call | solution.py:596

commit v9 on v8

--- a/solution.py
+++ b/solution.py
@@ -448,7 +448,7 @@
     first_half(1)
     held[...] = collect(2)
 
-    @pl.loop(3, 5)
+    @pl.loop(3, 6)
     def _(g):
         step(g)
 
@@ -459,7 +459,7 @@
     for k in range(1, GY):
         rows_copy(k).start()
 
-    @pl.loop(5, GROUPS)
+    @pl.loop(6, GROUPS)
     def _(g):
         step(g)
 

time: 45.3 us -> 45.3 us (level)
  no operation moved by 1% of the time
where the time goes in v9:
time: 45.3 us; the launch traced here: 45.2 us
  Pallas kernels  43.9 us (97%)
  between operations  1.29 us (3%)
    pallas_call x1, Pallas kernels, local(): pl.pallas_call(kernel, out_shape=(pltpu.VMEM((NB, BLK), F32), pltpu.VMEM(...  43 us

profile of v9, /device:TPU:1, one launch (start us, length us, event | category | flops | bytes accessed | tf_op | source)
XLA Modules:
  0.0 45.2 jit_solution(8688437541840388440)
XLA Ops:
  1.3 43.0 %shard_map.112 = (f32[32,128]{1,0:T(8,128)S(1)}, bf16[32,32,128]{2,1,0:T(8,128)(2,1)S(1)}, f32[27,32,32]{2,1,0:T(8,128)S(1)}) custom-call(bf16[32,32,128]{2,1,0:T(8,128)(2,1)} %feats_hbm.1, bf16[3,32,128]{2,1,0:T(8,128)(2,1)} %bitcast.5, s32[32,128]{1,0:T(8,128)} %base_hbm.1, s32[1,32]{1,0:T(1,128)} %bitcast.6, s32[1,1]{1,0:T(1,128)} %bitcast.4.count_hbm, ...), custom_call_target="tpu_custom_call" | custom-call | flops 8000000000 | bytes 2000000 | tf_op jit(solution)/shard_map/pallas_call | solution.py:542
  44.3 0.9 %shard_map.113 = (f32[32,128]{1,0:T(8,128)}, bf16[32,32,128]{2,1,0:T(8,128)(2,1)}, f32[27,32,32]{2,1,0:T(8,128)}) custom-call(f32[32,128]{1,0:T(8,128)S(1)} %get-tuple-element.6.pred, bf16[32,32,128]{2,1,0:T(8,128)(2,1)S(1)} %get-tuple-element.7.feats, f32[27,32,32]{2,1,0:T(8,128)S(1)} %get-tuple-element.8.conv), custom_call_target="tpu_custom_call" | custom-call | tf_op jit(solution)/shard_map/pallas_call | solution.py:596
